TPU v7x, 128 devices: a whole 4x4x4 slice. The times are simulated.
128 devices in a mesh: cuts: 8 (over z, y_hi), frame: 16 (over x, y_lo, core).
Axes of the slice: x: 4, y: 4 (y_hi: 2, y_lo: 2; y = y_hi * 2 + y_lo), z: 4, core: 2. Of those that a mesh axis runs over, the one named last changes fastest.
Arguments:
- cine_image: float32 [8, 16, 192, 384], P('cuts', 'frame'), may hold values from -6 to 6
- coil_maps: bfloat16 [8, 12, 192, 384], P('cuts'), may hold values from -4 to 4
- caipi_shift: int32 [8], P('cuts'), may hold values from 0 to 3
- line_mask: int32 [16, 192], P('frame'), may hold values 0 or 1
- measured: bfloat16 [8, 16, 12, 48, 384], P('cuts', 'frame'), may hold values from -6 to 6
- spatial_weight: float32 [32, 2, 3, 3], replicated, may hold values from -1.5 to 1.5
- temporal_weight: float32 [3, 32, 32], replicated, may hold values from -0.625 to 0.625
- project_weight: float32 [2, 32], replicated, may hold values from -1 to 1
Outputs:
- refined: float32 [8, 16, 192, 384], P('cuts', 'frame')
Inputs may be any that keep to these rules, and one draw needn't show every extreme that they name: `line_mask`: 1 where a line of a frame is sampled, else 0.
All inputs are finite; a program needn't handle non-finite values. No bound on the sum of `line_mask` on one device may be relied on, other than what follows from the above.
Results may differ from a plain program's by a relative error of at most 0.0023.
Values may be sent and summed in bfloat16 or wider, within the bound.
No kernel may reach another device: no remote copies, remote signals or barrier semaphores. Data moves between devices by JAX's collectives and lax.ppermute only.
A program may use at most 320 MiB of HBM per device.

v0:
```python
import math

import jax
import jax.numpy as jnp
import ml_dtypes
import numpy as np
from jax import lax
from jax.experimental import pallas as pl
from jax.experimental.pallas import tpu as pltpu
from jax.sharding import PartitionSpec as P


MB = 4
G = 4
PEERS = MB * G
SIDE = 192
COILS = 12
PER = COILS // MB
QR = SIDE // MB
SLAB = SIDE // PEERS
CHUNK = 8 * SLAB
MARK = 1e30
F32 = jnp.float32
BF16 = jnp.bfloat16
VMEM = pl.BlockSpec(memory_space=pltpu.VMEM)
SMEM = pl.BlockSpec(memory_space=pltpu.SMEM)
ANY = pl.BlockSpec(memory_space=pl.ANY)


def hi_lo(table):
    high = table.astype(ml_dtypes.bfloat16)
    low = (table - high.astype(np.float64)).astype(ml_dtypes.bfloat16)
    return high, low


def tables():
    at = np.arange(SIDE)
    angle = (at[:, None] * at[None, :] % SIDE) * (2.0 * math.pi / SIDE)
    cos = np.cos(angle) / math.sqrt(SIDE)
    sin = np.sin(angle) / math.sqrt(SIDE)
    return cos, sin


def width_matrix():
    cos, sin = tables()
    both = np.concatenate([np.concatenate([cos, -sin], 1), np.concatenate([sin, cos], 1)], 0)
    high, low = hi_lo(both)
    return np.concatenate([high, low], 0)


def folded(re, im):
    return np.concatenate([re[:, :128], re[:, 128:], im[:, 128:], im[:, :128]], 1)


def height_matrix():
    cos, sin = tables()
    real = folded(cos, sin)
    imag = folded(-sin, cos)
    both = np.concatenate([real, real, imag, imag], 0)
    return np.stack(hi_lo(both))


def line_index():
    lane = np.arange(2 * SIDE)
    line = np.where(lane < SIDE, lane, np.where(lane < 256, lane - 64, lane - 256))
    return line


def fold(re, im):
    return jnp.concatenate([re[:, :128], re[:, 128:], im[:, 128:], im[:, :128]], 1)


def dot_nt(a, b):
    return lax.dot_general(a, b, (((1,), (1,)), ((), ())), preferred_element_type=F32)


def dot_nn(a, b):
    return lax.dot_general(a, b, (((1,), (0,)), ((), ())), preferred_element_type=F32)


def pack_kernel(
    place_ref, x_ref, maps_ref, meas_ref, mask_ref, line_ref, w_ref, out_ref, maps_v, parts, stage, sem
):
    turn = place_ref[0]
    quarter = place_ref[1]
    member = place_ref[2]
    copy = pltpu.make_async_copy(maps_ref.at[pl.ds(member * PER, PER)], maps_v, sem)
    copy.start()

    def start(block):
        return pl.multiple_of(lax.rem(turn + block, MB) * QR, 16)

    lines = lax.broadcasted_iota(jnp.int32, (SIDE, 2 * SIDE), 0)
    select = (lines == line_ref[...] + quarter * QR).astype(F32).astype(BF16)
    mask8 = jnp.broadcast_to(mask_ref[...].astype(F32), (8, SIDE)).astype(BF16)
    sampled = dot_nn(mask8, select)[0:1] > 0.5
    for r in range(PER):
        rows = [
            meas_ref[PER * lax.rem(p + MB - quarter, MB) + r] for p in range(MB)
        ]
        both = dot_nt(w_ref[...], jnp.concatenate(rows, 0))
        re = both[0:SIDE] + both[2 * SIDE : 3 * SIDE]
        im = both[SIDE : 2 * SIDE] + both[3 * SIDE :]
        parts[4 + r] = jnp.where(sampled, fold(re, im), MARK)
    flipped = jnp.concatenate([x_ref[pl.ds(start(b), QR), :] for b in range(MB)], 0).T
    image = fold(flipped[:SIDE], flipped[SIDE:])
    high = image.astype(BF16).astype(F32)
    parts[3] = high
    parts[7] = image - high
    copy.wait()
    for r in range(PER):
        flipped = jnp.concatenate(
            [maps_v[r, pl.ds(start(b), QR), :] for b in range(MB)], 0
        ).astype(F32).T
        parts[r] = fold(flipped[:SIDE], flipped[SIDE:])
    for i in range(PEERS):
        for p in range(8):
            stage[i, SLAB * p : SLAB * (p + 1), :] = parts[p, SLAB * i : SLAB * (i + 1), :]
        out_ref[i] = stage[i].astype(BF16)


def slab_kernel(got_ref, a_ref, out_ref, xt, zs, ys):
    lane = lax.broadcasted_iota(jnp.int32, (40, 128), 1)
    left = lane < 64
    place = lax.broadcasted_iota(jnp.int32, (40, 2 * SIDE), 1)
    place = jnp.where(place < SIDE, place, jnp.where(place < 256, place - 64, place - 256))
    for i in range(PEERS):
        top = got_ref[i, 0:48, :].astype(F32)
        low = got_ref[i, 48:96, :].astype(F32)
        x = top[36:48] + low[36:48]
        x = jnp.concatenate([x, x, x, x[:4]], 0)
        mid = x[:, 128:256]
        turned = pltpu.roll(mid, 64, 1)
        xt[i, :, 0:128] = x[:, 0:128]
        xt[i, :, 128:256] = jnp.where(left, mid, turned)
        xt[i, :, 256:384] = jnp.where(left, -turned, mid)
        xt[i, :, 384:512] = x[:, 256:384]
    for j in range(MB):
        acc = [None] * G
        for m in range(MB):
            c = got_ref[m * G + j, 0:48, :].astype(F32)[0:40]
            c0, c1, c2 = c[:, 0:128], c[:, 128:256], c[:, 256:384]
            c1t = pltpu.roll(c1, 64, 1)
            for f in range(G):
                i = m * G + f
                x0, xa, xb, x2 = (xt[i, :, 128 * n : 128 * (n + 1)] for n in range(4))
                o0 = c0 * x0 - c2 * x2
                o1 = c1 * xa + c1t * xb
                o2 = c0 * x2 + c2 * x0
                if m > 0:
                    o0 += zs[40 * f : 40 * f + 40, 0:128]
                    o1 += zs[40 * f : 40 * f + 40, 128:256]
                    o2 += zs[40 * f : 40 * f + 40, 256:384]
                zs[40 * f : 40 * f + 40, 0:128] = o0
                zs[40 * f : 40 * f + 40, 128:256] = o1
                zs[40 * f : 40 * f + 40, 256:384] = o2
        off = QR * ((MB - j) % MB)
        pieces = ((off, 128), (off + 128, 64), (2 * SIDE + off + 128, 64), (2 * SIDE + off, 128))
        a_hi = jnp.concatenate([a_ref[0, s : s + n, :] for s, n in pieces], 0)
        a_lo = jnp.concatenate([a_ref[1, s : s + n, :] for s, n in pieces], 0)
        z = zs[...]
        zh = z.astype(BF16)
        zl = (z - zh.astype(F32)).astype(BF16)
        rows = 40 * G
        both = dot_nt(jnp.concatenate([zh, zl], 0), a_hi)
        zk = both[:rows] + both[rows:] + dot_nt(zh, a_lo)
        rest = []
        for f in range(G):
            t = None
            for p in range(MB):
                q = (p - j) % MB
                src = got_ref[q * G + f, 48:96, :].astype(F32)[0:40]
                t = src if t is None else jnp.where(place >= p * QR, src, t)
            rest.append(jnp.where(t > 0.1 * MARK, 0.0, zk[40 * f : 40 * f + 40] - t))
        r = jnp.concatenate(rest, 0)
        rh = r.astype(BF16)
        rl = (r - rh.astype(F32)).astype(BF16)
        both = dot_nn(jnp.concatenate([rh, rl], 0), a_hi)
        ys[j] = both[:rows] + both[rows:] + dot_nn(rh, a_lo)
    for m in range(MB):
        acc = [None] * G
        for j in range(MB):
            c = got_ref[m * G + j, 0:48, :].astype(F32)[0:40]
            c0, c1, c2 = c[:, 0:128], c[:, 128:256], c[:, 256:384]
            c1t = pltpu.roll(c1, 64, 1)
            ca = jnp.where(left, c1, c1t)
            cb = jnp.where(left, c1t, -c1)
            for f in range(G):
                y = ys[j, 40 * f : 40 * f + 40, :]
                y0, y1, y2 = y[:, 0:128], y[:, 128:256], y[:, 256:384]
                o = jnp.concatenate(
                    [c0 * y0 + c2 * y2, ca * y1 + cb * pltpu.roll(y1, 64, 1), c0 * y2 - c2 * y0], 1
                )
                acc[f] = o if acc[f] is None else acc[f] + o
        for f in range(G):
            total = acc[f][0:12] + acc[f][12:24] + acc[f][24:36]
            high = total.astype(BF16).astype(F32)
            out_ref[m * G + f] = jnp.concatenate([high, total - high], 0).astype(BF16)


def update_kernel(place_ref, x_ref, back_ref, out_ref, turned, grad):
    turn = place_ref[0]
    for i in range(PEERS):
        both = back_ref[i].astype(F32)
        turned[SLAB * i : SLAB * (i + 1), :] = both[:SLAB] + both[SLAB:]
    re = turned[:, 0:SIDE]
    im = jnp.concatenate([turned[:, 256:384], turned[:, 192:256]], 1)
    grad[...] = jnp.concatenate([re, im], 0).T
    for b in range(MB):
        at = pl.multiple_of(lax.rem(b + MB - turn, MB) * QR, 16)
        rows = slice(b * QR, (b + 1) * QR)
        out_ref[rows, :] = x_ref[rows, :] - 0.5 * grad[pl.ds(at, QR), :]


def refine_kernel(prior_ref, own_ref, later_ref, m_ref, p_ref, out_ref, lay):
    zeros = jnp.zeros((18, 8, SIDE), F32)
    lay[:, 0:8, :] = zeros
    lay[:, 192:200, :] = zeros
    column = lax.broadcasted_iota(jnp.int32, (SIDE, SIDE), 1)
    for t, ref in enumerate((prior_ref, own_ref, later_ref)):
        u = ref[...]
        for p in range(2):
            for b in range(3):
                by = (1 - b - SIDE * p) % (2 * SIDE)
                v = (pltpu.roll(u, by, 1) if by else u)[:, :SIDE]
                if b == 0:
                    v = jnp.where(column == 0, 0.0, v)
                if b == 2:
                    v = jnp.where(column == SIDE - 1, 0.0, v)
                lay[(t * 2 + p) * 3 + b, 1 : SIDE + 1, :] = v

    def step(i, carry):
        at = pl.multiple_of(i * 8, 8)
        window = lay[:, pl.ds(at, 16), :].reshape(18 * 16, SIDE)
        high = window.astype(BF16)
        low = (window - high.astype(F32)).astype(BF16)
        mix = dot_nn(m_ref[...], jnp.concatenate([high, low, high], 0))
        re = None
        im = None
        for o in range(32):
            v = jnp.maximum(mix[8 * o : 8 * o + 8], 0.0)
            re = v * p_ref[0, o] if re is None else re + v * p_ref[0, o]
            im = v * p_ref[1, o] if im is None else im + v * p_ref[1, o]
        out_ref[pl.ds(at, 8), :] = own_ref[pl.ds(at, 8), :] + jnp.concatenate([re, im], 1)
        return carry

    lax.fori_loop(0, SIDE // 8, step, 0)


def params(mib):
    return pltpu.CompilerParams(vmem_limit_bytes=mib * 1024 * 1024)


def groups(cuts, frames):
    found = {}
    for c in range(cuts):
        for f in range(frames):
            found.setdefault((c % (cuts // MB), f // G), []).append(c * frames + f)
    return list(found.values())


def mixing_matrix(spatial_weight, temporal_weight):
    joint = jnp.einsum(
        "toi,ipab->otpab", temporal_weight, spatial_weight, precision=lax.Precision.HIGHEST
    )
    gap = np.arange(16)[None, :] - np.arange(8)[:, None]
    matrix = 0.0
    for a in range(3):
        hit = jnp.asarray((gap == a).astype(np.float32))
        matrix = matrix + joint[:, None, :, :, a, :, None] * hit[None, :, None, None, None, :]
    matrix = matrix.reshape(256, 18 * 16)
    high = matrix.astype(BF16)
    low = (matrix - high.astype(F32)).astype(BF16)
    return jnp.concatenate([high, high, low], 1)


def on_device(
    cine_image,
    coil_maps,
    caipi_shift,
    line_mask,
    measured,
    spatial_weight,
    temporal_weight,
    project_weight,
):
    cuts = lax.axis_size("cuts")
    frames = lax.axis_size("frame")
    quarter = lax.axis_index("cuts") // (cuts // MB)
    member = lax.axis_index("frame") % G
    place = jnp.stack([caipi_shift[0], quarter, member]).astype(jnp.int32)
    image = cine_image[0, 0]
    send = pl.pallas_call(
        pack_kernel,
        out_shape=jax.ShapeDtypeStruct((PEERS, CHUNK, 2 * SIDE), BF16),
        in_specs=[SMEM, VMEM, ANY, VMEM, VMEM, VMEM, VMEM],
        out_specs=VMEM,
        scratch_shapes=[
            pltpu.VMEM((PER, SIDE, 2 * SIDE), BF16),
            pltpu.VMEM((8, SIDE, 2 * SIDE), F32),
            pltpu.VMEM((PEERS, CHUNK, 2 * SIDE), F32),
            pltpu.SemaphoreType.DMA,
        ],
        compiler_params=params(32),
        name="pack",
    )(
        place,
        image,
        coil_maps[0],
        measured[0, 0],
        line_mask,
        jnp.asarray((line_index() % QR).astype(np.int32))[None],
        jnp.asarray(width_matrix()),
    )
    where = groups(cuts, frames)
    got = lax.all_to_all(send, ("cuts", "frame"), 0, 0, axis_index_groups=where)
    slab = pl.pallas_call(
        slab_kernel,
        out_shape=jax.ShapeDtypeStruct((PEERS, 2 * SLAB, 2 * SIDE), BF16),
        in_specs=[VMEM, VMEM],
        out_specs=VMEM,
        scratch_shapes=[
            pltpu.VMEM((PEERS, 40, 512), F32),
            pltpu.VMEM((40 * G, 2 * SIDE), F32),
            pltpu.VMEM((MB, 40 * G, 2 * SIDE), F32),
        ],
        compiler_params=params(32),
        name="slab",
    )(got, jnp.asarray(height_matrix()))
    back = lax.all_to_all(slab, ("cuts", "frame"), 0, 0, axis_index_groups=where)
    updated = pl.pallas_call(
        update_kernel,
        out_shape=jax.ShapeDtypeStruct((SIDE, 2 * SIDE), F32),
        in_specs=[SMEM, VMEM, VMEM],
        out_specs=VMEM,
        scratch_shapes=[pltpu.VMEM((SIDE, 2 * SIDE), F32), pltpu.VMEM((SIDE, 2 * SIDE), F32)],
        compiler_params=params(16),
        name="update",
    )(place, image, back)
    forward = [(i, (i + 1) % frames) for i in range(frames)]
    prior = lax.ppermute(updated, "frame", forward)
    later = lax.ppermute(updated, "frame", [(b, a) for a, b in forward])
    refined = pl.pallas_call(
        refine_kernel,
        out_shape=jax.ShapeDtypeStruct((SIDE, 2 * SIDE), F32),
        in_specs=[VMEM, VMEM, VMEM, VMEM, SMEM],
        out_specs=VMEM,
        scratch_shapes=[pltpu.VMEM((18, 208, SIDE), F32)],
        compiler_params=params(32),
        name="refine",
    )(prior, updated, later, mixing_matrix(spatial_weight, temporal_weight), project_weight)
    return refined[None, None]


def solution(mesh):
    return jax.shard_map(
        on_device,
        mesh=mesh,
        in_specs=(
            P("cuts", "frame", None, None),
            P("cuts", None, None, None),
            P("cuts"),
            P("frame", None),
            P("cuts", "frame", None, None, None),
            P(),
            P(),
            P(),
        ),
        out_specs=P("cuts", "frame", None, None),
        check_vma=False,
    )
```

profile of v0, /device:TPU:0, one launch (start us, length us, event | category | flops | bytes accessed | tf_op | source)
XLA Modules:
  0.0 74.3 jit_solution(8658493913195295308)
XLA Ops:
  0.7 1.5 %copy-done.1 = bf16[1,12,192,384]{3,2,1,0:T(8,128)(2,1)S(1)} copy-done((bf16[1,12,192,384]{3,2,1,0:T(8,128)(2,1)S(1)}, bf16[1,12,192,384]{3,2,1,0:T(8,128)(2,1)}, u32[]{:S(2)}) %copy-start.1) | copy-done | bytes 1769496
  2.2 1.0 %copy-done.2 = f32[1,1,192,384]{3,2,1,0:T(8,128)S(1)} copy-done((f32[1,1,192,384]{3,2,1,0:T(8,128)S(1)}, f32[1,1,192,384]{3,2,1,0:T(8,128)}, u32[]{:S(2)}) %copy-start.2) | copy-done | bytes 294936
  3.2 1.1 %copy-done.5 = bf16[768,384]{1,0:T(8,128)(2,1)S(1)} copy-done((bf16[768,384]{1,0:T(8,128)(2,1)S(1)}, bf16[768,384]{1,0:T(8,128)(2,1)}, u32[]{:S(2)}) %copy-start.5) | copy-done | bytes 589848
  4.3 1.0 %copy-done.6 = bf16[1,1,12,48,384]{4,3,2,1,0:T(8,128)(2,1)S(1)} copy-done((bf16[1,1,12,48,384]{4,3,2,1,0:T(8,128)(2,1)S(1)}, bf16[1,1,12,48,384]{4,3,2,1,0:T(8,128)(2,1)}, u32[]{:S(2)}) %copy-start.6) | copy-done | bytes 442392
  5.3 0.7 copy-done.7
  5.9 0.7 copy-done.8
  6.6 3.3 %pack.1 = bf16[16,96,384]{2,1,0:T(8,128)(2,1)} custom-call(s32[3]{0:T(128)S(1)} %pad_add_fusion.place_ref, f32[192,384]{1,0:T(8,128)S(1)} %bitcast.21, bf16[12,192,384]{2,1,0:T(8,128)(2,1)S(1)} %bitcast.20, bf16[12,48,384]{2,1,0:T(8,128)(2,1)S(1)} %bitcast.23, s32[1,192]{1,0:T(1,128)S(1)} %copy-done.8, s32[1,384]{1,0:T(1,128)S(1)} %copy-done.7, ...), custom_call_target="tpu_custom_call" | custom-call | tf_op jit(solution)/shard_map/pack/pallas_call | solution.py:293
  9.9 6.7 %all-to-all-start = ((bf16[16,96,384]{2,1,0:T(8,128)(2,1)}), bf16[16,96,384]{2,1,0:T(8,128)(2,1)S(1)}, u32[]{:S(2)}, u32[]{:S(2)}) async-start(bf16[16,96,384]{2,1,0:T(8,128)(2,1)} %pack.1), calls=%async_computation | async-start | bytes 2359296 | tf_op jit(solution)/shard_map/all_to_all | solution.py:316
  16.6 0.3 convolution_bitcast_fusion
  16.9 0.1 copy.20
  17.1 0.1 copy.22
  17.2 0.1 copy.21
  17.4 17.3 %all-to-all-done.got_ref = bf16[16,96,384]{2,1,0:T(8,128)(2,1)S(1)} async-done(((bf16[16,96,384]{2,1,0:T(8,128)(2,1)}), bf16[16,96,384]{2,1,0:T(8,128)(2,1)S(1)}, u32[]{:S(2)}, u32[]{:S(2)}) %all-to-all-start) | async-done | bytes 1179680 | tf_op jit(solution)/shard_map/all_to_all | solution.py:316
  34.7 4.4 %slab.1 = bf16[16,24,384]{2,1,0:T(8,128)(2,1)} custom-call(bf16[16,96,384]{2,1,0:T(8,128)(2,1)S(1)} %all-to-all-done.got_ref, bf16[2,768,384]{2,1,0:T(8,128)(2,1)S(1)} %copy-done.4), custom_call_target="tpu_custom_call" | custom-call | tf_op jit(solution)/shard_map/slab/pallas_call | solution.py:317
  39.0 3.5 %all-to-all-start.1 = ((bf16[16,24,384]{2,1,0:T(8,128)(2,1)}), bf16[16,24,384]{2,1,0:T(8,128)(2,1)S(1)}, u32[]{:S(2)}, u32[]{:S(2)}) async-start(bf16[16,24,384]{2,1,0:T(8,128)(2,1)} %slab.1), calls=%async_computation.1 | async-start | bytes 589824 | tf_op jit(solution)/shard_map/all_to_all | solution.py:330
  42.6 2.4 %multiply_add_fusion = f32[32,8,3,2,3,16]{5,4,3,2,1,0:T(4,128)} fusion(f32[8,16]{1,0:T(8,128)S(1)} %copy-done.11, f32[32,3,2,3]{3,2,1,0:T(2,128)S(1)} %copy.22, f32[8,16]{1,0:T(8,128)S(1)} %copy-done.12, f32[32,3,2,3]{3,2,1,0:T(2,128)S(1)} %copy.21, f32[8,16]{1,0:T(8,128)S(1)} %copy-done.13, f32[32,3,2,3]{3,2,1,0:T(2,128)S(1)} %copy.20), kind=kLoop, calls=%fused_computation | loop fusion | flops 368640 | bytes 303360 | tf_op jit(solution)/shard_map/add | solution.py:270
  45.1 3.5 %add.20 = f32[256,288]{1,0:T(8,128)S(1)} reshape(f32[32,8,3,2,3,16]{5,4,3,2,1,0:T(4,128)} %multiply_add_fusion) | data formatting | bytes 589824 | tf_op jit(solution)/shard_map/add | solution.py:270
  48.5 2.4 %all-to-all-done.1.back_ref = bf16[16,24,384]{2,1,0:T(8,128)(2,1)S(1)} async-done(((bf16[16,24,384]{2,1,0:T(8,128)(2,1)}), bf16[16,24,384]{2,1,0:T(8,128)(2,1)S(1)}, u32[]{:S(2)}, u32[]{:S(2)}) %all-to-all-start.1) | async-done | bytes 294944 | tf_op jit(solution)/shard_map/all_to_all | solution.py:330
  51.0 0.8 %update.1.own_ref = f32[192,384]{1,0:T(8,128)S(1)} custom-call(s32[3]{0:T(128)S(1)} %pad_add_fusion.place_ref, f32[192,384]{1,0:T(8,128)S(1)} %bitcast.22, bf16[16,24,384]{2,1,0:T(8,128)(2,1)S(1)} %all-to-all-done.1.back_ref), custom_call_target="tpu_custom_call" | custom-call | tf_op jit(solution)/shard_map/update/pallas_call | solution.py:331
  51.8 2.7 %collective-permute-start.1 = (f32[192,384]{1,0:T(8,128)S(1)}, f32[192,384]{1,0:T(8,128)S(1)}, u32[]{:S(2)}, u32[]{:S(2)}) collective-permute-start(f32[192,384]{1,0:T(8,128)S(1)} %update.1.own_ref), channel_id=1, source_target_pairs={{1,0},{2,1},{3,2},{4,3},{5,4},{6,5},{7,6},{8,7},{9,8},{10,9},{11,1... | collective-permute-start | bytes 884744 | tf_op jit(solution)/shard_map/ppermute | solution.py:342
  54.5 0.2 pad_maximum_fusion.m_ref
  54.7 4.0 %collective-permute-done.1.later_ref = f32[192,384]{1,0:T(8,128)S(1)} collective-permute-done((f32[192,384]{1,0:T(8,128)S(1)}, f32[192,384]{1,0:T(8,128)S(1)}, u32[]{:S(2)}, u32[]{:S(2)}) %collective-permute-start.1) | collective-permute-done | bytes 294944 | tf_op jit(solution)/shard_map/ppermute | solution.py:342
  58.7 4.0 %collective-permute-done.prior_ref = f32[192,384]{1,0:T(8,128)S(1)} collective-permute-done((f32[192,384]{1,0:T(8,128)S(1)}, f32[192,384]{1,0:T(8,128)S(1)}, u32[]{:S(2)}, u32[]{:S(2)}) %collective-permute-start) | collective-permute-done | bytes 294944 | tf_op jit(solution)/shard_map/ppermute | solution.py:341
  62.7 11.6 %refine.1 = f32[192,384]{1,0:T(8,128)} custom-call(f32[192,384]{1,0:T(8,128)S(1)} %collective-permute-done.prior_ref, f32[192,384]{1,0:T(8,128)S(1)} %update.1.own_ref, f32[192,384]{1,0:T(8,128)S(1)} %collective-permute-done.1.later_ref, bf16[256,864]{1,0:T(8,128)(2,1)S(1)} %pad_maximum_fusion.m_ref, f32[2,32]{1,0:T(2,128)S(1)} %copy-done.9), custom_call_target="tpu_custom_call" | custom-call | tf_op jit(solution)/shard_map/refine/pallas_call | solution.py:343
  (26 shorter events, 0.2 us)
Async XLA Ops:
  0.0 16.6 %copy-start = (f32[3,32,32]{2,1,0:T(8,128)S(1)}, f32[3,32,32]{2,1,0:T(8,128)}, u32[]{:S(2)}) copy-start(f32[3,32,32]{2,1,0:T(8,128)} %param.20) | copy-start | bytes 36868
  0.7 1.5 %copy-start.1 = (bf16[1,12,192,384]{3,2,1,0:T(8,128)(2,1)S(1)}, bf16[1,12,192,384]{3,2,1,0:T(8,128)(2,1)}, u32[]{:S(2)}) copy-start(bf16[1,12,192,384]{3,2,1,0:T(8,128)(2,1)} %param.15) | copy-start | bytes 5308420
  2.2 1.0 %copy-start.2 = (f32[1,1,192,384]{3,2,1,0:T(8,128)S(1)}, f32[1,1,192,384]{3,2,1,0:T(8,128)}, u32[]{:S(2)}) copy-start(f32[1,1,192,384]{3,2,1,0:T(8,128)} %param.14) | copy-start | bytes 884740
  3.2 1.1 %copy-start.5 = (bf16[768,384]{1,0:T(8,128)(2,1)S(1)}, bf16[768,384]{1,0:T(8,128)(2,1)}, u32[]{:S(2)}) copy-start(bf16[768,384]{1,0:T(8,128)(2,1)} %constant.48.clone.w_ref) | copy-start | bytes 1769476
  4.3 1.0 %copy-start.6 = (bf16[1,1,12,48,384]{4,3,2,1,0:T(8,128)(2,1)S(1)}, bf16[1,1,12,48,384]{4,3,2,1,0:T(8,128)(2,1)}, u32[]{:S(2)}) copy-start(bf16[1,1,12,48,384]{4,3,2,1,0:T(8,128)(2,1)} %param.18) | copy-start | bytes 1327108
  5.3 0.7 copy-start.7
  5.9 0.7 copy-start.8
  6.6 10.0 %copy-start.10 = (f32[32,2,3,3]{0,1,3,2:T(2,128)S(1)}, f32[32,2,3,3]{0,1,3,2:T(2,128)}, u32[]{:S(2)}) copy-start(f32[32,2,3,3]{0,1,3,2:T(2,128)} %param.19) | copy-start | bytes 6916
  6.6 28.0 %copy-start.4 = (bf16[2,768,384]{2,1,0:T(8,128)(2,1)S(1)}, bf16[2,768,384]{2,1,0:T(8,128)(2,1)}, u32[]{:S(2)}) copy-start(bf16[2,768,384]{2,1,0:T(8,128)(2,1)} %constant.49.clone.a_ref) | copy-start | bytes 3538948
  9.9 32.7 %copy-start.11 = (f32[8,16]{1,0:T(8,128)S(1)}, f32[8,16]{1,0:T(8,128)}, u32[]{:S(2)}) copy-start(f32[8,16]{1,0:T(8,128)} %constant.52.clone) | copy-start | bytes 1540
  9.9 32.7 %copy-start.12 = (f32[8,16]{1,0:T(8,128)S(1)}, f32[8,16]{1,0:T(8,128)}, u32[]{:S(2)}) copy-start(f32[8,16]{1,0:T(8,128)} %constant.51.clone) | copy-start | bytes 1540
  9.9 32.7 %copy-start.13 = (f32[8,16]{1,0:T(8,128)S(1)}, f32[8,16]{1,0:T(8,128)}, u32[]{:S(2)}) copy-start(f32[8,16]{1,0:T(8,128)} %constant.50.clone) | copy-start | bytes 1540
  9.9 24.7 %all-to-all-start = ((bf16[16,96,384]{2,1,0:T(8,128)(2,1)}), bf16[16,96,384]{2,1,0:T(8,128)(2,1)S(1)}, u32[]{:S(2)}, u32[]{:S(2)}) async-start(bf16[16,96,384]{2,1,0:T(8,128)(2,1)} %pack.1), calls=%async_computation | async-start | bytes 2359296 | tf_op jit(solution)/shard_map/all_to_all | solution.py:316
  39.0 11.9 %all-to-all-start.1 = ((bf16[16,24,384]{2,1,0:T(8,128)(2,1)}), bf16[16,24,384]{2,1,0:T(8,128)(2,1)S(1)}, u32[]{:S(2)}, u32[]{:S(2)}) async-start(bf16[16,24,384]{2,1,0:T(8,128)(2,1)} %slab.1), calls=%async_computation.1 | async-start | bytes 589824 | tf_op jit(solution)/shard_map/all_to_all | solution.py:330
  42.6 8.3 %copy-start.3 = (f32[1,1,192,384]{3,2,1,0:T(8,128)S(1)}, f32[1,1,192,384]{3,2,1,0:T(8,128)}, u32[]{:S(2)}) copy-start(f32[1,1,192,384]{3,2,1,0:T(8,128)} %param.14) | copy-start | bytes 884740
  45.1 17.6 %copy-start.9 = (f32[2,32]{1,0:T(2,128)S(1)}, f32[2,32]{1,0:T(2,128)}, u32[]{:S(2)}) copy-start(f32[2,32]{1,0:T(2,128)} %p_ref.1) | copy-start | bytes 772
  51.8 6.9 %collective-permute-start.1 = (f32[192,384]{1,0:T(8,128)S(1)}, f32[192,384]{1,0:T(8,128)S(1)}, u32[]{:S(2)}, u32[]{:S(2)}) collective-permute-start(f32[192,384]{1,0:T(8,128)S(1)} %update.1.own_ref), channel_id=1, source_target_pairs={{1,0},{2,1},{3,2},{4,3},{5,4},{6,5},{7,6},{8,7},{9,8},{10,9},{11,1... | collective-permute-start | bytes 884744 | tf_op jit(solution)/shard_map/ppermute | solution.py:342
  54.4 8.3 %collective-permute-start = (f32[192,384]{1,0:T(8,128)S(1)}, f32[192,384]{1,0:T(8,128)S(1)}, u32[]{:S(2)}, u32[]{:S(2)}) collective-permute-start(f32[192,384]{1,0:T(8,128)S(1)} %update.1.own_ref), channel_id=1, source_target_pairs={{0,1},{1,2},{2,3},{3,4},{4,5},{5,6},{6,7},{7,8},{8,9},{9,10},{10,1... | collective-permute-start | bytes 884744 | tf_op jit(solution)/shard_map/ppermute | solution.py:341
where the time goes:
time: 74.9 us; the launch traced here: 74.3 us
  waiting for transfers between devices  27.7 us (37%)
  Pallas kernels  20.1 us (27%)
  starting transfers between devices  12.9 us (17%)
  local copies, waits for them, and re-layouts  9.81 us (13%)
  other arithmetic  2.77 us (4%)
  between operations  0.82 us (1%)
    all_to_all x1, waiting for transfers between devices, on_device(): got = lax.all_to_all(send, ('cuts', 'frame'), 0, 0, axis_index_groups=where)  17.3 us
    pallas_call x1, Pallas kernels, on_device(): pl.pallas_call(refine_kernel, out_shape=jax.ShapeDtypeStruct((SIDE, 2 * S...  11.6 us
    all_to_all x1, starting transfers between devices, on_device(): got = lax.all_to_all(send, ('cuts', 'frame'), 0, 0, axis_index_groups=where)  6.65 us
    unnamed x28, local copies, waits for them, and re-layouts  5.92 us
    pallas_call x1, Pallas kernels, on_device(): pl.pallas_call(slab_kernel, out_shape=jax.ShapeDtypeStruct((PEERS, 2 * SL...  4.38 us
    ppermute x1, waiting for transfers between devices, on_device(): later = lax.ppermute(updated, 'frame', [(b, a) for a, b in forward])  4.02 us
    ppermute x1, waiting for transfers between devices, on_device(): prior = lax.ppermute(updated, 'frame', forward)  3.97 us
    all_to_all x1, starting transfers between devices, on_device(): lax.all_to_all(slab, ('cuts', 'frame'), 0, 0, axis_index_groups=where)  3.54 us
  transfers between devices with their start and end apart: 4, of which 4 were waited for; matrix products, arithmetic and copies ran while one was open for 9% of the time, Pallas kernels for 0%

commit v1 on v0

v1 whole, which is shorter than its diff:
```python
import math

import jax
import jax.numpy as jnp
import ml_dtypes
import numpy as np
from jax import lax
from jax.experimental import pallas as pl
from jax.experimental.pallas import tpu as pltpu
from jax.sharding import PartitionSpec as P


MB = 4
G = 4
PEERS = MB * G
SIDE = 192
COILS = 12
PER = COILS // MB
QR = SIDE // MB
SLAB = SIDE // PEERS
CHUNK = 8 * SLAB
MARK = 1e30
F32 = jnp.float32
BF16 = jnp.bfloat16
VMEM = pl.BlockSpec(memory_space=pltpu.VMEM)
SMEM = pl.BlockSpec(memory_space=pltpu.SMEM)
ANY = pl.BlockSpec(memory_space=pl.ANY)
HBM = pl.BlockSpec(memory_space=pltpu.HBM)


def hi_lo(table):
    high = table.astype(ml_dtypes.bfloat16)
    low = (table - high.astype(np.float64)).astype(ml_dtypes.bfloat16)
    return high, low


def tables():
    at = np.arange(SIDE)
    angle = (at[:, None] * at[None, :] % SIDE) * (2.0 * math.pi / SIDE)
    cos = np.cos(angle) / math.sqrt(SIDE)
    sin = np.sin(angle) / math.sqrt(SIDE)
    return cos, sin


def width_matrix():
    cos, sin = tables()
    both = np.concatenate([np.concatenate([cos, -sin], 1), np.concatenate([sin, cos], 1)], 0)
    high, low = hi_lo(both)
    return np.concatenate([high, low], 0)


def folded(re, im):
    return np.concatenate([re[:, :128], re[:, 128:], im[:, 128:], im[:, :128]], 1)


def height_matrix():
    cos, sin = tables()
    real = folded(cos, sin)
    imag = folded(-sin, cos)
    both = np.concatenate([real, real, imag, imag], 0)
    return np.stack(hi_lo(both))


def line_pieces(group):
    off = QR * ((MB - group) % MB)
    return ((off, 128), (off + 128, 64), (2 * SIDE + off + 128, 64), (2 * SIDE + off, 128))


def slab_matrices():
    table = height_matrix()
    turned = []
    for j in range(MB):
        rows = np.concatenate([table[:, s : s + n] for s, n in line_pieces(j)], 1)
        turned.append(np.swapaxes(rows, 1, 2))
    return np.stack(turned + [table[:, : 2 * SIDE], table[:, 2 * SIDE :]])


def fold(re, im):
    return jnp.concatenate([re[:, :128], re[:, 128:], im[:, 128:], im[:, :128]], 1)


def dot_nt(a, b):
    return lax.dot_general(a, b, (((1,), (1,)), ((), ())), preferred_element_type=F32)


def dot_nn(a, b):
    return lax.dot_general(a, b, (((1,), (0,)), ((), ())), preferred_element_type=F32)


def pack_kernel(
    turn_ref, x_hbm, maps_hbm, meas_hbm, mask_hbm, w_hbm, out_hbm,
    x_ref, maps_ref, meas_ref, mask_ref, w_ref, parts, out_ref, sems, out_sems,
):
    turn = turn_ref[0]
    quarter = lax.axis_index("cuts") // (lax.axis_size("cuts") // MB)
    member = lax.rem(lax.axis_index("frame"), G)
    loads = [
        pltpu.make_async_copy(src, dst, sems.at[n])
        for n, (src, dst) in enumerate(
            (
                (x_hbm, x_ref),
                (maps_hbm.at[pl.ds(member * PER, PER)], maps_ref),
                (mask_hbm, mask_ref),
                (w_hbm, w_ref),
                (meas_hbm, meas_ref),
            )
        )
    ]
    for load in loads:
        load.start()

    def start(block):
        return pl.multiple_of(lax.rem(turn + block, MB) * QR, 16)

    loads[0].wait()
    flipped = jnp.concatenate([x_ref[pl.ds(start(b), QR), :] for b in range(MB)], 0).T
    image = fold(flipped[:SIDE], flipped[SIDE:])
    high = image.astype(BF16).astype(F32)
    parts[3] = high
    parts[7] = image - high
    loads[1].wait()
    for r in range(PER):
        flipped = jnp.concatenate(
            [maps_ref[r, pl.ds(start(b), QR), :] for b in range(MB)], 0
        ).astype(F32).T
        parts[r] = fold(flipped[:SIDE], flipped[SIDE:])
    lane = lax.broadcasted_iota(jnp.int32, (SIDE, 2 * SIDE), 1)
    line = jnp.where(lane < SIDE, lane, jnp.where(lane < 256, lane - 64, lane - 256))
    for _ in range(MB - 1):
        line = jnp.where(line >= QR, line - QR, line)
    lines = lax.broadcasted_iota(jnp.int32, (SIDE, 2 * SIDE), 0)
    select = (lines == line + quarter * QR).astype(F32).astype(BF16)
    loads[2].wait()
    mask8 = jnp.broadcast_to(mask_ref[...].astype(F32), (8, SIDE)).astype(BF16)
    sampled = dot_nn(mask8, select)[0:1] > 0.5
    loads[3].wait()
    loads[4].wait()
    for r in range(PER):
        rows = [meas_ref[PER * lax.rem(p + MB - quarter, MB) + r] for p in range(MB)]
        both = dot_nt(w_ref[...], jnp.concatenate(rows, 0))
        re = both[0:SIDE] + both[2 * SIDE : 3 * SIDE]
        im = both[SIDE : 2 * SIDE] + both[3 * SIDE :]
        parts[4 + r] = jnp.where(sampled, fold(re, im), MARK)
    for i in range(PEERS):
        tiles = [parts[p, 8 * i : 8 * i + 8, :] for p in range(8)]
        out_ref[i, 0:64, :] = jnp.concatenate(tiles, 0).astype(BF16)
        tiles = [parts[p, 128 + 4 * i : 132 + 4 * i, :] for p in range(8)]
        out_ref[i, 64:96, :] = jnp.concatenate(tiles, 0).astype(BF16)
        pltpu.make_async_copy(out_ref.at[i], out_hbm.at[i], out_sems.at[i]).start()
    for i in range(PEERS):
        pltpu.make_async_copy(out_ref.at[i], out_hbm.at[i], out_sems.at[i]).wait()


def cut(value):
    return [value[8 * t : 8 * t + 8] for t in range(value.shape[0] // 8)]


def slab_kernel(got_ref, a_ref, out_hbm, xs, cs, zs, ys, out_ref, sems):
    left = lax.broadcasted_iota(jnp.int32, (8, 128), 1) < 64
    lane = lax.broadcasted_iota(jnp.int32, (8, 128), 1)
    low16 = (lane < 16) | ((lane >= 64) & (lane < 80))
    for i in range(PEERS):
        main = got_ref[i, 0:32, :].astype(F32)
        half = got_ref[i, 64:80, :].astype(F32)
        x8 = main[24:32] + got_ref[i, 32:64, :].astype(F32)[24:32]
        x4 = (half[8:16] + got_ref[i, 80:96, :].astype(F32)[8:16])[4:8]
        for t, x in enumerate((x8, jnp.concatenate([x4, x4], 0))):
            mid = x[:, 128:256]
            turned = pltpu.roll(mid, 64, 1)
            xs[i, t, :, 0:128] = x[:, 0:128]
            xs[i, t, :, 128:256] = jnp.where(left, mid, turned)
            xs[i, t, :, 256:384] = jnp.where(left, -turned, mid)
            xs[i, t, :, 384:512] = x[:, 256:384]
        for t, c in enumerate(cut(main[0:24]) + cut(half)):
            cs[i, t, :, 0:384] = c
            cs[i, t, :, 384:512] = pltpu.roll(c[:, 128:256], 64, 1)

    def gather(j):
        for t in range(5):
            acc = [None] * G
            for m in range(MB):
                c0, c1, c2, c1t = (cs[m * G + j, t, :, 128 * n : 128 * n + 128] for n in range(4))
                for f in range(G):
                    x0, xa, xb, x2 = (
                        xs[m * G + f, t // 3, :, 128 * n : 128 * n + 128] for n in range(4)
                    )
                    o = (c0 * x0 - c2 * x2, c1 * xa + c1t * xb, c0 * x2 + c2 * x0)
                    acc[f] = o if m == 0 else tuple(p + q for p, q in zip(acc[f], o))
            for f in range(G):
                for n in range(3):
                    zs[j, 40 * f + 8 * t : 40 * f + 8 * t + 8, 128 * n : 128 * n + 128] = acc[f][n]

    def matrices(j):
        return [
            jnp.concatenate(
                [
                    a_ref[MB + s // (2 * SIDE), h, s % (2 * SIDE) : s % (2 * SIDE) + n, :]
                    for s, n in line_pieces(j)
                ],
                0,
            )
            for h in range(2)
        ]

    def triple(value, high, low):
        top = value.astype(BF16)
        rest = (value - top.astype(F32)).astype(BF16)
        return dot_nn(
            jnp.concatenate([top, rest, top], 1), jnp.concatenate([high, high, low], 0)
        )

    def residual(j, zk):
        out = []
        for f in range(G):
            sources = []
            for p in range(MB):
                i = ((p - j) % MB) * G + f
                main = got_ref[i, 32:64, :].astype(F32)[0:24]
                sources.append(cut(main) + cut(got_ref[i, 80:96, :].astype(F32)))
            for t in range(5):
                row = 40 * f + 8 * t
                s0, s1, s2, s3 = (source[t] for source in sources)
                outer = [
                    jnp.where(lane < 48, s0[:, n], jnp.where(lane < 96, s1[:, n], s2[:, n]))
                    for n in (slice(0, 128), slice(256, 384))
                ]
                mid = jnp.where(low16, s2[:, 128:256], s3[:, 128:256])
                target = jnp.concatenate([outer[0], mid, outer[1]], 1)
                out.append(jnp.where(target > 0.1 * MARK, 0.0, zk[row : row + 8] - target))
        return jnp.concatenate(out, 0)

    gather(0)
    for j in range(MB):
        zk = triple(zs[j], a_ref[j, 0], a_ref[j, 1])
        if j + 1 < MB:
            gather(j + 1)
        y = triple(residual(j, zk), *matrices(j))
        ys[j, :, 0:384] = y
        ys[j, :, 384:512] = pltpu.roll(y[:, 128:256], 64, 1)

    for m in range(MB):
        sums = []
        for tiles in ((0, 1, 2), (3,), (4,)):
            acc = [None] * G
            for t in tiles:
                for j in range(MB):
                    c0, c1, c2, c1t = (
                        cs[m * G + j, t, :, 128 * n : 128 * n + 128] for n in range(4)
                    )
                    ca = jnp.where(left, c1, c1t)
                    cb = jnp.where(left, c1t, -c1)
                    for f in range(G):
                        row = 40 * f + 8 * t
                        y0, y1, y2, y1t = (
                            ys[j, row : row + 8, 128 * n : 128 * n + 128] for n in range(4)
                        )
                        o = (c0 * y0 + c2 * y2, ca * y1 + cb * y1t, c0 * y2 - c2 * y0)
                        acc[f] = o if acc[f] is None else tuple(p + q for p, q in zip(acc[f], o))
            sums.append([jnp.concatenate(o, 1) for o in acc])
        for f in range(G):
            i = m * G + f
            main, third, fourth = (part[f] for part in sums)
            half = third[0:4] + third[4:8] + fourth[0:4]
            main_hi = main.astype(BF16).astype(F32)
            half_hi = half.astype(BF16).astype(F32)
            out_ref[i] = jnp.concatenate(
                [main_hi, main - main_hi, half_hi, half - half_hi], 0
            ).astype(BF16)
            pltpu.make_async_copy(out_ref.at[i], out_hbm.at[i], sems.at[i]).start()
    for i in range(PEERS):
        pltpu.make_async_copy(out_ref.at[i], out_hbm.at[i], sems.at[i]).wait()


def update_kernel(turn_ref, x_ref, back_ref, out_ref, edge_ref, turned, grad):
    turn = turn_ref[0]
    for i in range(PEERS):
        both = back_ref[i].astype(F32)
        turned[8 * i : 8 * i + 8, :] = both[0:8] + both[8:16]
        turned[128 + 4 * i : 132 + 4 * i, :] = both[16:20] + both[20:24]
    re = turned[:, 0:SIDE]
    im = jnp.concatenate([turned[:, 256:384], turned[:, 192:256]], 1)
    grad[...] = jnp.concatenate([re, im], 0).T
    for b in range(MB):
        at = pl.multiple_of(lax.rem(b + MB - turn, MB) * QR, 16)
        rows = slice(b * QR, (b + 1) * QR)
        u = x_ref[rows, :] - 0.5 * grad[pl.ds(at, QR), :]
        out_ref[rows, :] = u
        edge_ref[rows, :] = u.astype(BF16)


def spread(lay, frames):
    zeros = jnp.zeros((lay.shape[0], 8, SIDE), F32)
    lay[:, 0:8, :] = zeros
    lay[:, 192:200, :] = zeros
    column = lax.broadcasted_iota(jnp.int32, (SIDE, SIDE), 1)
    for t, u in enumerate(frames):
        for p in range(2):
            for b in range(3):
                by = (1 - b - SIDE * p) % (2 * SIDE)
                v = (pltpu.roll(u, by, 1) if by else u)[:, :SIDE]
                if b == 0:
                    v = jnp.where(column == 0, 0.0, v)
                if b == 2:
                    v = jnp.where(column == SIDE - 1, 0.0, v)
                lay[(t * 2 + p) * 3 + b, 1 : SIDE + 1, :] = v


def dot_exact(a, b):
    return lax.dot_general(
        a, b, (((1,), (0,)), ((), ())), precision=lax.Precision.HIGHEST, preferred_element_type=F32
    )


def mixing_matrices(temporal_ref, spatial_ref):
    odd = lax.rem(lax.axis_index("frame"), 2) == 1
    before, after = temporal_ref[0], temporal_ref[2]
    joint = [
        dot_exact(side, spatial_ref[...])
        for side in (
            jnp.where(odd, before, after),
            temporal_ref[1],
            jnp.where(odd, after, before),
        )
    ]

    def build(blocks):
        width = 96 * len(blocks)
        lane = lax.broadcasted_iota(jnp.int32, (18, width), 1)
        entry = lax.broadcasted_iota(jnp.int32, (18, width), 0)
        block = sum((lane >= 96 * n).astype(jnp.int32) for n in range(1, len(blocks)))
        channel = (lane - 96 * block) >> 4
        part = (channel >= 3).astype(jnp.int32)
        at = lax.broadcasted_iota(jnp.int32, (256, width), 1)
        gap = (at & 15) - (lax.broadcasted_iota(jnp.int32, (256, width), 0) & 7)
        total = jnp.zeros((256, width), F32)
        for a in range(3):
            table = (entry == part * 6 + a * 3 + channel).astype(F32)
            picked = None
            for n in sorted({frame for frame, _ in blocks}):
                mine = sum(
                    jnp.where(block == k, table, 0.0)
                    for k, (frame, _) in enumerate(blocks)
                    if frame == n
                )
                term = dot_exact(joint[n], mine)
                picked = term if picked is None else picked + term
            wide = jnp.broadcast_to(picked[:, None, :], (32, 8, width)).reshape(256, width)
            total = jnp.where(gap == a, wide, total)
        high = total.astype(BF16).astype(F32)
        for k, (_, rest) in enumerate(blocks):
            if rest:
                inside = (at >= 96 * k) & (at < 96 * k + 96)
                high = jnp.where(inside, total - high, high)
        return high.astype(BF16)

    near = build(((0, False), (0, True), (1, False), (1, False), (1, True)))
    far = build(((2, False), (2, True)))
    return near, far


def near_kernel(core_ref, own_ref, temporal_ref, spatial_ref, acc_ref, far_ref, lay, m_ref):
    m_ref[...], far_ref[...] = mixing_matrices(temporal_ref, spatial_ref)
    spread(lay, [core_ref[...].astype(F32), own_ref[...]])
    for i in range(SIDE // 8):
        near = lay[0:6, 8 * i : 8 * i + 16, :].reshape(6 * 16, SIDE).astype(BF16)
        window = lay[6:12, 8 * i : 8 * i + 16, :].reshape(6 * 16, SIDE)
        high = window.astype(BF16)
        low = (window - high.astype(F32)).astype(BF16)
        acc_ref[i] = dot_nn(m_ref[...], jnp.concatenate([near, near, high, low, high], 0))


def refine_kernel(chip_ref, own_ref, acc_ref, m_ref, p_ref, out_hbm, lay, out_ref, sems):
    spread(lay, [chip_ref[...].astype(F32)])
    steps = SIDE // 8
    copies = []
    for i in range(steps):
        window = lay[:, 8 * i : 8 * i + 16, :].reshape(6 * 16, SIDE).astype(BF16)
        mix = dot_nn(m_ref[...], jnp.concatenate([window, window], 0)) + acc_ref[i]
        re = None
        im = None
        for o in range(32):
            v = jnp.maximum(mix[8 * o : 8 * o + 8], 0.0)
            re = v * p_ref[0, o] if re is None else re + v * p_ref[0, o]
            im = v * p_ref[1, o] if im is None else im + v * p_ref[1, o]
        rows = slice(8 * i, 8 * i + 8)
        out_ref[rows, :] = own_ref[rows, :] + jnp.concatenate([re, im], 1)
        if i % 6 == 5:
            part = pl.ds(8 * (i - 5), 48)
            copies.append(
                pltpu.make_async_copy(out_ref.at[part], out_hbm.at[part], sems.at[i // 6])
            )
            copies[-1].start()
    for copy in copies:
        copy.wait()


def params(mib):
    return pltpu.CompilerParams(vmem_limit_bytes=mib * 1024 * 1024)


def groups(cuts, frames):
    found = {}
    for c in range(cuts):
        for f in range(frames):
            found.setdefault((c % (cuts // MB), f // G), []).append(c * frames + f)
    return list(found.values())


def cost(flops, moved):
    return pl.CostEstimate(flops=flops, bytes_accessed=moved, transcendentals=0)


def on_device(
    cine_image,
    coil_maps,
    caipi_shift,
    line_mask,
    measured,
    spatial_weight,
    temporal_weight,
    project_weight,
):
    cuts = lax.axis_size("cuts")
    frames = lax.axis_size("frame")
    image = cine_image[0, 0]
    send = pl.pallas_call(
        pack_kernel,
        out_shape=jax.ShapeDtypeStruct((PEERS, CHUNK, 2 * SIDE), BF16),
        in_specs=[SMEM, HBM, HBM, HBM, HBM, HBM],
        out_specs=HBM,
        scratch_shapes=[
            pltpu.VMEM((SIDE, 2 * SIDE), F32),
            pltpu.VMEM((PER, SIDE, 2 * SIDE), BF16),
            pltpu.VMEM((COILS, QR, 2 * SIDE), BF16),
            pltpu.VMEM((1, SIDE), jnp.int32),
            pltpu.VMEM((4 * SIDE, 2 * SIDE), BF16),
            pltpu.VMEM((8, SIDE, 2 * SIDE), F32),
            pltpu.VMEM((PEERS, CHUNK, 2 * SIDE), BF16),
            pltpu.SemaphoreType.DMA((5,)),
            pltpu.SemaphoreType.DMA((PEERS,)),
        ],
        compiler_params=params(58),
        name="pack",
    )(
        caipi_shift,
        image,
        coil_maps[0],
        measured[0, 0],
        line_mask,
        jnp.asarray(width_matrix()),
    )
    where = groups(cuts, frames)
    got = lax.all_to_all(send, ("cuts", "frame"), 0, 0, axis_index_groups=where)
    slab = pl.pallas_call(
        slab_kernel,
        out_shape=jax.ShapeDtypeStruct((PEERS, 2 * SLAB, 2 * SIDE), BF16),
        in_specs=[VMEM, VMEM],
        out_specs=HBM,
        scratch_shapes=[
            pltpu.VMEM((PEERS, 2, 8, 512), F32),
            pltpu.VMEM((PEERS, 5, 8, 512), F32),
            pltpu.VMEM((MB, 40 * G, 2 * SIDE), F32),
            pltpu.VMEM((MB, 40 * G, 512), F32),
            pltpu.VMEM((PEERS, 2 * SLAB, 2 * SIDE), BF16),
            pltpu.SemaphoreType.DMA((PEERS,)),
        ],
        compiler_params=params(32),
        name="slab",
    )(got, jnp.asarray(slab_matrices()))
    back = lax.all_to_all(slab, ("cuts", "frame"), 0, 0, axis_index_groups=where)
    updated, edge = pl.pallas_call(
        update_kernel,
        out_shape=(
            jax.ShapeDtypeStruct((SIDE, 2 * SIDE), F32),
            jax.ShapeDtypeStruct((SIDE, 2 * SIDE), BF16),
        ),
        in_specs=[SMEM, VMEM, VMEM],
        out_specs=(VMEM, VMEM),
        scratch_shapes=[pltpu.VMEM((SIDE, 2 * SIDE), F32), pltpu.VMEM((SIDE, 2 * SIDE), F32)],
        compiler_params=params(16),
        name="update",
    )(caipi_shift, image, back)
    on_chip = lax.ppermute(edge, "frame", [(i, i ^ 1) for i in range(frames)])
    off_chip = lax.ppermute(
        edge, "frame", [(i, (i + 1) % frames if i % 2 else (i - 1) % frames) for i in range(frames)]
    )
    mixed, far_matrix = pl.pallas_call(
        near_kernel,
        out_shape=(
            jax.ShapeDtypeStruct((SIDE // 8, 256, SIDE), F32),
            jax.ShapeDtypeStruct((256, 192), BF16),
        ),
        in_specs=[VMEM, VMEM, VMEM, VMEM],
        out_specs=(VMEM, VMEM),
        scratch_shapes=[pltpu.VMEM((12, 208, SIDE), F32), pltpu.VMEM((256, 480), BF16)],
        compiler_params=params(24),
        cost_estimate=cost(24 * 2 * 256 * 480 * 192, 6 * 2**20),
        name="near",
    )(on_chip, updated, temporal_weight, spatial_weight.reshape(32, 18))
    refined = pl.pallas_call(
        refine_kernel,
        out_shape=jax.ShapeDtypeStruct((SIDE, 2 * SIDE), F32),
        in_specs=[VMEM, VMEM, VMEM, VMEM, SMEM],
        out_specs=HBM,
        scratch_shapes=[
            pltpu.VMEM((6, 208, SIDE), F32),
            pltpu.VMEM((SIDE, 2 * SIDE), F32),
            pltpu.SemaphoreType.DMA((4,)),
        ],
        compiler_params=params(24),
        name="refine",
    )(off_chip, updated, mixed, far_matrix, project_weight)
    return refined[None, None]


def solution(mesh):
    return jax.shard_map(
        on_device,
        mesh=mesh,
        in_specs=(
            P("cuts", "frame", None, None),
            P("cuts", None, None, None),
            P("cuts"),
            P("frame", None),
            P("cuts", "frame", None, None, None),
            P(),
            P(),
            P(),
        ),
        out_specs=P("cuts", "frame", None, None),
        check_vma=False,
    )
```

time: 74.9 us -> 54.3 us (0.72)
  blocking collectives: 0 us -> 35.5 us
  waiting for transfers between devices: 27.7 us -> 0.86 us
  starting transfers between devices: 12.9 us -> 3.03 us
  local copies, waits for them, and re-layouts: 9.81 us -> 0.13 us
  Pallas kernels: 20.1 us -> 13.9 us
  other arithmetic: 2.77 us -> 0 us
    all_to_all x0 -> x2, blocking collectives: none -> 35.5 us  [the longest x1 24.5 us: on_device(): got = lax.all_to_all(send, ('cuts', 'frame'), 0, 0, axis_index_groups=where)]
    all_to_all x2 -> x0, waiting for transfers between devices: 19.7 us -> none  [the longest x1 17.3 us: on_device(): got = lax.all_to_all(send, ('cuts', 'frame'), 0, 0, axis_index_groups=where)]
    all_to_all x2 -> x0, starting transfers between devices: 10.2 us -> none  [the longest x1 6.65 us: on_device(): got = lax.all_to_all(send, ('cuts', 'frame'), 0, 0, axis_index_groups=where)]
    pallas_call x1, Pallas kernels: 11.6 us -> 3.04 us  [on_device(): pl.pallas_call(refine_kernel, out_shape=jax.ShapeDtypeStruct((SIDE, 2 * S...]
    ppermute x2, waiting for transfers between devices: 7.99 us -> 0.86 us  [the longest x1 0.85 us: on_device(): lax.ppermute(edge, 'frame', [(i, (i + 1) % frames if i % 2 else (i - 1) %...]
    unnamed x28 -> x11, local copies, waits for them, and re-layouts: 5.92 us -> 0.03 us
    add x1 -> x0, local copies, waits for them, and re-layouts: 3.46 us -> none  [mixing_matrix(): matrix + joint[:, None, :, :, a, :, None] * hit[None, :, None, None, None...]
    add x1 -> x0, other arithmetic: 2.44 us -> none  [mixing_matrix(): matrix + joint[:, None, :, :, a, :, None] * hit[None, :, None, None, None...]
  transfers between devices with their start and end apart: 4 -> 2, of which waited for: 4 -> 1; matrix products, arithmetic and copies ran while one was open for 9% -> 0% of each run, Pallas kernels for 0% -> 5%
where the time goes in v1:
time: 54.3 us; the launch traced here: 54.1 us
  blocking collectives  35.5 us (65%)
  Pallas kernels  13.9 us (26%)
  starting transfers between devices  3.03 us (6%)
  waiting for transfers between devices  0.86 us (2%)
  between operations  0.72 us (1%)
    all_to_all x1, blocking collectives, on_device(): got = lax.all_to_all(send, ('cuts', 'frame'), 0, 0, axis_index_groups=where)  24.5 us
    all_to_all x1, blocking collectives, on_device(): lax.all_to_all(slab, ('cuts', 'frame'), 0, 0, axis_index_groups=where)  11 us
    pallas_call x1, Pallas kernels, on_device(): pl.pallas_call(pack_kernel, out_shape=jax.ShapeDtypeStruct((PEERS, CHUNK,...  3.96 us
    pallas_call x1, Pallas kernels, on_device(): pl.pallas_call(slab_kernel, out_shape=jax.ShapeDtypeStruct((PEERS, 2 * SL...  3.75 us
    pallas_call x1, Pallas kernels, on_device(): pl.pallas_call(refine_kernel, out_shape=jax.ShapeDtypeStruct((SIDE, 2 * S...  3.04 us
    ppermute x1, starting transfers between devices, on_device(): lax.ppermute(edge, 'frame', [(i, (i + 1) % frames if i % 2 else (i - 1) %...  2.95 us
    pallas_call x1, Pallas kernels, on_device(): pl.pallas_call(near_kernel, out_shape=(jax.ShapeDtypeStruct((SIDE // 8, 2...  2.89 us
  transfers between devices with their start and end apart: 2, of which 1 were waited for; matrix products, arithmetic and copies ran while one was open for 0% of the time, Pallas kernels for 5%

profile of v1, /device:TPU:0, one launch (start us, length us, event | category | flops | bytes accessed | tf_op | source)
XLA Modules:
  0.0 54.1 jit_solution(14232397295451073354)
XLA Ops:
  0.7 0.0 copy-start
  0.7 4.0 %pack.1 = bf16[16,96,384]{2,1,0:T(8,128)(2,1)} custom-call(s32[1]{0:T(128)S(6)} %copy.14.turn_ref, f32[192,384]{1,0:T(8,128)} %bitcast.6, bf16[12,192,384]{2,1,0:T(8,128)(2,1)} %bitcast.8, bf16[12,48,384]{2,1,0:T(8,128)(2,1)} %bitcast.9, s32[1,192]{1,0:T(1,128)} %mask_hbm.1, bf16[768,384]{1,0:T(8,128)(2,1)} %constant.4.clone.w_hbm), custom_call_target="tpu_custom_call" | custom-call | tf_op jit(solution)/shard_map/pack/pallas_call | solution.py:426
  4.6 24.5 %all_to_all.10.got_ref = bf16[16,96,384]{2,1,0:T(8,128)(2,1)S(1)} all-to-all(bf16[16,96,384]{2,1,0:T(8,128)(2,1)} %pack.1), channel_id=1, replica_groups={{0,1,2,3,32,33,34,35,64,65,66,67,96,97,98,99},{4,5,6,7,36,37,38,39,68,6..., dimensions={0} | all-to-all | bytes 2359296 | tf_op jit(solution)/shard_map/all_to_all | solution.py:453
  29.1 0.0 copy-done
  29.1 0.0 copy-start.1
  29.1 0.0 copy-start.4
  29.1 0.0 copy-start.3
  29.1 3.8 %slab.1 = bf16[16,24,384]{2,1,0:T(8,128)(2,1)S(1)} custom-call(bf16[16,96,384]{2,1,0:T(8,128)(2,1)S(1)} %all_to_all.10.got_ref, bf16[6,2,384,384]{3,2,1,0:T(8,128)(2,1)S(1)} %copy-done), custom_call_target="tpu_custom_call" | custom-call | tf_op jit(solution)/shard_map/slab/pallas_call | solution.py:454
  32.9 11.0 %all_to_all.11.back_ref = bf16[16,24,384]{2,1,0:T(8,128)(2,1)S(1)} all-to-all(bf16[16,24,384]{2,1,0:T(8,128)(2,1)S(1)} %slab.1), channel_id=1, replica_groups={{0,1,2,3,32,33,34,35,64,65,66,67,96,97,98,99},{4,5,6,7,36,37,38,39,68,6..., dimensions={0} | all-to-all | bytes 589824 | tf_op jit(solution)/shard_map/all_to_all | solution.py:470
  43.9 0.0 copy-done.1
  43.9 0.3 update.1
  44.1 0.1 collective-permute-start.1
  44.2 2.9 %collective-permute-start = (bf16[192,384]{1,0:T(8,128)(2,1)S(1)}, bf16[192,384]{1,0:T(8,128)(2,1)S(1)}, u32[]{:S(2)}, u32[]{:S(2)}) collective-permute-start(bf16[192,384]{1,0:T(8,128)(2,1)S(1)} %get-tuple-element.9), channel_id=1, source_target_pairs={{0,15},{1,2},{2,1},{3,4},{4,3},{5,6},{6,5},{7,8},{8,7},{9,10},{10,... | collective-permute-start | bytes 442376 | tf_op jit(solution)/shard_map/ppermute | solution.py:484
  47.2 0.0 copy-done.4
  47.2 0.1 copy.13.spatial_ref
  47.3 0.0 collective-permute-done.1.core_ref
  47.3 0.0 copy-done.3
  47.3 0.0 copy-start.2
  47.3 2.9 %near.1 = (f32[24,256,192]{2,1,0:T(8,128)S(1)}, bf16[256,192]{1,0:T(8,128)(2,1)S(1)}) custom-call(bf16[192,384]{1,0:T(8,128)(2,1)S(1)} %collective-permute-done.1.core_ref, f32[192,384]{1,0:T(8,128)S(1)} %get-tuple-element.10.own_ref, f32[3,32,32]{2,1,0:T(8,128)S(1)} %copy-done.3, f32[32,18]{1,0:T(8,128)S(1)} %copy.13.spatial_ref), custom_call_target="tpu_custom_call" | custom-call | flops 1132462080 | bytes 6291456 | tf_op jit(solution)/shard_map/near/pallas_call | solution.py:487
  50.2 0.9 %collective-permute-done.chip_ref = bf16[192,384]{1,0:T(8,128)(2,1)S(1)} collective-permute-done((bf16[192,384]{1,0:T(8,128)(2,1)S(1)}, bf16[192,384]{1,0:T(8,128)(2,1)S(1)}, u32[]{:S(2)}, u32[]{:S(2)}) %collective-permute-start) | collective-permute-done | bytes 147488 | tf_op jit(solution)/shard_map/ppermute | solution.py:484
  51.1 0.0 copy-done.2
  51.1 3.0 %refine.1 = f32[192,384]{1,0:T(8,128)} custom-call(bf16[192,384]{1,0:T(8,128)(2,1)S(1)} %collective-permute-done.chip_ref, f32[192,384]{1,0:T(8,128)S(1)} %get-tuple-element.10.own_ref, f32[24,256,192]{2,1,0:T(8,128)S(1)} %get-tuple-element.11.acc_ref, bf16[256,192]{1,0:T(8,128)(2,1)S(1)} %get-tuple-element.12.m_ref, f32[2,32]{1,0:T(2,128)S(1)} %copy-done.2), custom_call_target="tpu_custom_call" | custom-call | tf_op jit(solution)/shard_map/refine/pallas_call | solution.py:500
  (2 shorter events, 0.0 us)
Async XLA Ops:
  0.7 28.5 %copy-start = (bf16[6,2,384,384]{3,2,1,0:T(8,128)(2,1)S(1)}, bf16[6,2,384,384]{3,2,1,0:T(8,128)(2,1)}, u32[]{:S(2)}) copy-start(bf16[6,2,384,384]{3,2,1,0:T(8,128)(2,1)} %constant.5.clone.a_ref) | copy-start | bytes 10616836
  29.1 14.8 %copy-start.1 = (f32[1,1,192,384]{3,2,1,0:T(8,128)S(1)}, f32[1,1,192,384]{3,2,1,0:T(8,128)}, u32[]{:S(2)}) copy-start(f32[1,1,192,384]{3,2,1,0:T(8,128)} %param.10) | copy-start | bytes 884740
  29.1 18.1 %copy-start.4 = (f32[32,2,3,3]{0,1,3,2:T(2,128)S(1)}, f32[32,2,3,3]{0,1,3,2:T(2,128)}, u32[]{:S(2)}) copy-start(f32[32,2,3,3]{0,1,3,2:T(2,128)} %param.15) | copy-start | bytes 6916
  29.1 18.2 %copy-start.3 = (f32[3,32,32]{2,1,0:T(8,128)S(1)}, f32[3,32,32]{2,1,0:T(8,128)}, u32[]{:S(2)}) copy-start(f32[3,32,32]{2,1,0:T(8,128)} %temporal_ref.1) | copy-start | bytes 36868
  44.1 3.2 %collective-permute-start.1 = (bf16[192,384]{1,0:T(8,128)(2,1)S(1)}, bf16[192,384]{1,0:T(8,128)(2,1)S(1)}, u32[]{:S(2)}, u32[]{:S(2)}) collective-permute-start(bf16[192,384]{1,0:T(8,128)(2,1)S(1)} %get-tuple-element.9), channel_id=1, source_target_pairs={{0,1},{1,0},{2,3},{3,2},{4,5},{5,4},{6,7},{7,6},{8,9},{9,8},{10,11... | collective-permute-start | bytes 442376 | tf_op jit(solution)/shard_map/ppermute | solution.py:483
  44.2 6.8 %collective-permute-start = (bf16[192,384]{1,0:T(8,128)(2,1)S(1)}, bf16[192,384]{1,0:T(8,128)(2,1)S(1)}, u32[]{:S(2)}, u32[]{:S(2)}) collective-permute-start(bf16[192,384]{1,0:T(8,128)(2,1)S(1)} %get-tuple-element.9), channel_id=1, source_target_pairs={{0,15},{1,2},{2,1},{3,4},{4,3},{5,6},{6,5},{7,8},{8,7},{9,10},{10,... | collective-permute-start | bytes 442376 | tf_op jit(solution)/shard_map/ppermute | solution.py:484
  47.3 3.8 %copy-start.2 = (f32[2,32]{1,0:T(2,128)S(1)}, f32[2,32]{1,0:T(2,128)}, u32[]{:S(2)}) copy-start(f32[2,32]{1,0:T(2,128)} %p_ref.1) | copy-start | bytes 772

commit v2 on v1

--- a/solution.py
+++ b/solution.py
@@ -18,7 +18,7 @@
 PER = COILS // MB
 QR = SIDE // MB
 SLAB = SIDE // PEERS
-CHUNK = 8 * SLAB
+CHUNK = 88
 MARK = 1e30
 F32 = jnp.float32
 BF16 = jnp.bfloat16
@@ -88,10 +88,9 @@
 
 
 def pack_kernel(
-    turn_ref, x_hbm, maps_hbm, meas_hbm, mask_hbm, w_hbm, out_hbm,
-    x_ref, maps_ref, meas_ref, mask_ref, w_ref, parts, out_ref, sems, out_sems,
+    turn_hbm, x_hbm, maps_hbm, meas_hbm, mask_hbm, w_hbm, out_hbm,
+    turn_ref, x_ref, maps_ref, meas_ref, mask_ref, w_ref, parts, out_ref, sems, out_sems,
 ):
-    turn = turn_ref[0]
     quarter = lax.axis_index("cuts") // (lax.axis_size("cuts") // MB)
     member = lax.rem(lax.axis_index("frame"), G)
     loads = [
@@ -103,11 +102,14 @@
                 (mask_hbm, mask_ref),
                 (w_hbm, w_ref),
                 (meas_hbm, meas_ref),
+                (turn_hbm, turn_ref),
             )
         )
     ]
     for load in loads:
         load.start()
+    loads[5].wait()
+    turn = turn_ref[0]
 
     def start(block):
         return pl.multiple_of(lax.rem(turn + block, MB) * QR, 16)
@@ -142,10 +144,9 @@
         im = both[SIDE : 2 * SIDE] + both[3 * SIDE :]
         parts[4 + r] = jnp.where(sampled, fold(re, im), MARK)
     for i in range(PEERS):
-        tiles = [parts[p, 8 * i : 8 * i + 8, :] for p in range(8)]
-        out_ref[i, 0:64, :] = jnp.concatenate(tiles, 0).astype(BF16)
-        tiles = [parts[p, 128 + 4 * i : 132 + 4 * i, :] for p in range(8)]
-        out_ref[i, 64:96, :] = jnp.concatenate(tiles, 0).astype(BF16)
+        tiles = [parts[p, 8 * i : 8 * i + 8, :] for p in range(7)]
+        tiles += [parts[p, 128 + 4 * i : 132 + 4 * i, :] for p in range(8)]
+        out_ref[i] = jnp.concatenate(tiles, 0).astype(BF16)
         pltpu.make_async_copy(out_ref.at[i], out_hbm.at[i], out_sems.at[i]).start()
     for i in range(PEERS):
         pltpu.make_async_copy(out_ref.at[i], out_hbm.at[i], out_sems.at[i]).wait()
@@ -160,18 +161,16 @@
     lane = lax.broadcasted_iota(jnp.int32, (8, 128), 1)
     low16 = (lane < 16) | ((lane >= 64) & (lane < 80))
     for i in range(PEERS):
-        main = got_ref[i, 0:32, :].astype(F32)
-        half = got_ref[i, 64:80, :].astype(F32)
-        x8 = main[24:32] + got_ref[i, 32:64, :].astype(F32)[24:32]
-        x4 = (half[8:16] + got_ref[i, 80:96, :].astype(F32)[8:16])[4:8]
-        for t, x in enumerate((x8, jnp.concatenate([x4, x4], 0))):
+        tiles = cut(got_ref[i].astype(F32))
+        x4 = (tiles[8] + tiles[10])[4:8]
+        for t, x in enumerate((tiles[3], jnp.concatenate([x4, x4], 0))):
             mid = x[:, 128:256]
             turned = pltpu.roll(mid, 64, 1)
             xs[i, t, :, 0:128] = x[:, 0:128]
             xs[i, t, :, 128:256] = jnp.where(left, mid, turned)
             xs[i, t, :, 256:384] = jnp.where(left, -turned, mid)
             xs[i, t, :, 384:512] = x[:, 256:384]
-        for t, c in enumerate(cut(main[0:24]) + cut(half)):
+        for t, c in enumerate(tiles[0:3] + tiles[7:9]):
             cs[i, t, :, 0:384] = c
             cs[i, t, :, 384:512] = pltpu.roll(c[:, 128:256], 64, 1)
 
@@ -215,8 +214,8 @@
             sources = []
             for p in range(MB):
                 i = ((p - j) % MB) * G + f
-                main = got_ref[i, 32:64, :].astype(F32)[0:24]
-                sources.append(cut(main) + cut(got_ref[i, 80:96, :].astype(F32)))
+                tiles = cut(got_ref[i].astype(F32))
+                sources.append(tiles[4:7] + tiles[9:11])
             for t in range(5):
                 row = 40 * f + 8 * t
                 s0, s1, s2, s3 = (source[t] for source in sources)
@@ -271,6 +270,18 @@
         pltpu.make_async_copy(out_ref.at[i], out_hbm.at[i], sems.at[i]).wait()
 
 
+def lost_part(x, mask, maps_ref):
+    power = None
+    for c in range(COILS):
+        maps = maps_ref[c].astype(F32)
+        power = maps * maps if power is None else power + maps * maps
+    share = jnp.sum(mask.astype(F32), axis=1, keepdims=True) * (1.0 / SIDE)
+    power = power + pltpu.roll(power, SIDE, 1)
+    lane = lax.broadcasted_iota(jnp.int32, (SIDE, 2 * SIDE), 1)
+    rounded = (lane < 128) | ((lane >= SIDE) & (lane < SIDE + 128))
+    return share * power * jnp.where(rounded, x - x.astype(BF16).astype(F32), 0.0)
+
+
 def update_kernel(turn_ref, x_ref, back_ref, out_ref, edge_ref, turned, grad):
     turn = turn_ref[0]
     for i in range(PEERS):
@@ -358,9 +369,14 @@
     return near, far
 
 
-def near_kernel(core_ref, own_ref, temporal_ref, spatial_ref, acc_ref, far_ref, lay, m_ref):
+def near_kernel(
+    core_ref, own_ref, x_ref, mask_ref, temporal_ref, spatial_ref, maps_ref,
+    acc_ref, far_ref, out_ref, lay, m_ref,
+):
     m_ref[...], far_ref[...] = mixing_matrices(temporal_ref, spatial_ref)
-    spread(lay, [core_ref[...].astype(F32), own_ref[...]])
+    own = own_ref[...] - 0.5 * lost_part(x_ref[...], mask_ref[...], maps_ref)
+    out_ref[...] = own
+    spread(lay, [core_ref[...].astype(F32), own])
     for i in range(SIDE // 8):
         near = lay[0:6, 8 * i : 8 * i + 16, :].reshape(6 * 16, SIDE).astype(BF16)
         window = lay[6:12, 8 * i : 8 * i + 16, :].reshape(6 * 16, SIDE)
@@ -426,9 +442,10 @@
     send = pl.pallas_call(
         pack_kernel,
         out_shape=jax.ShapeDtypeStruct((PEERS, CHUNK, 2 * SIDE), BF16),
-        in_specs=[SMEM, HBM, HBM, HBM, HBM, HBM],
+        in_specs=[HBM, HBM, HBM, HBM, HBM, HBM],
         out_specs=HBM,
         scratch_shapes=[
+            pltpu.SMEM((1,), jnp.int32),
             pltpu.VMEM((SIDE, 2 * SIDE), F32),
             pltpu.VMEM((PER, SIDE, 2 * SIDE), BF16),
             pltpu.VMEM((COILS, QR, 2 * SIDE), BF16),
@@ -436,7 +453,7 @@
             pltpu.VMEM((4 * SIDE, 2 * SIDE), BF16),
             pltpu.VMEM((8, SIDE, 2 * SIDE), F32),
             pltpu.VMEM((PEERS, CHUNK, 2 * SIDE), BF16),
-            pltpu.SemaphoreType.DMA((5,)),
+            pltpu.SemaphoreType.DMA((6,)),
             pltpu.SemaphoreType.DMA((PEERS,)),
         ],
         compiler_params=params(58),
@@ -484,19 +501,31 @@
     off_chip = lax.ppermute(
         edge, "frame", [(i, (i + 1) % frames if i % 2 else (i - 1) % frames) for i in range(frames)]
     )
-    mixed, far_matrix = pl.pallas_call(
+    mixed, far_matrix, own = pl.pallas_call(
         near_kernel,
         out_shape=(
             jax.ShapeDtypeStruct((SIDE // 8, 256, SIDE), F32),
             jax.ShapeDtypeStruct((256, 192), BF16),
+            jax.ShapeDtypeStruct((SIDE, 2 * SIDE), F32),
         ),
-        in_specs=[VMEM, VMEM, VMEM, VMEM],
-        out_specs=(VMEM, VMEM),
-        scratch_shapes=[pltpu.VMEM((12, 208, SIDE), F32), pltpu.VMEM((256, 480), BF16)],
+        in_specs=[VMEM, VMEM, VMEM, VMEM, VMEM, VMEM, VMEM],
+        out_specs=(VMEM, VMEM, VMEM),
+        scratch_shapes=[
+            pltpu.VMEM((12, 208, SIDE), F32),
+            pltpu.VMEM((256, 480), BF16),
+        ],
         compiler_params=params(24),
         cost_estimate=cost(24 * 2 * 256 * 480 * 192, 6 * 2**20),
         name="near",
-    )(on_chip, updated, temporal_weight, spatial_weight.reshape(32, 18))
+    )(
+        on_chip,
+        updated,
+        image,
+        line_mask,
+        temporal_weight,
+        spatial_weight.reshape(32, 18),
+        coil_maps[0],
+    )
     refined = pl.pallas_call(
         refine_kernel,
         out_shape=jax.ShapeDtypeStruct((SIDE, 2 * SIDE), F32),
@@ -509,7 +538,7 @@
         ],
         compiler_params=params(24),
         name="refine",
-    )(off_chip, updated, mixed, far_matrix, project_weight)
+    )(off_chip, own, mixed, far_matrix, project_weight)
     return refined[None, None]
 
 

time: 54.3 us -> 53.4 us (0.983)
  blocking collectives: 35.5 us -> 34.5 us
    all_to_all x1, blocking collectives: 24.5 us -> 23.5 us  [on_device(): got = lax.all_to_all(send, ('cuts', 'frame'), 0, 0, axis_index_groups=where)]
  transfers between devices with their start and end apart: 2 -> 2, of which waited for: 1 -> 1; matrix products, arithmetic and copies ran while one was open for 0% -> 0% of each run, Pallas kernels for 5% -> 6%
where the time goes in v2:
time: 53.4 us; the launch traced here: 53.2 us
  blocking collectives  34.5 us (65%)
  Pallas kernels  14.2 us (27%)
  starting transfers between devices  3.04 us (6%)
  between operations  0.75 us (1%)
  waiting for transfers between devices  0.65 us (1%)
    all_to_all x1, blocking collectives, on_device(): got = lax.all_to_all(send, ('cuts', 'frame'), 0, 0, axis_index_groups=where)  23.5 us
    all_to_all x1, blocking collectives, on_device(): lax.all_to_all(slab, ('cuts', 'frame'), 0, 0, axis_index_groups=where)  11 us
    pallas_call x1, Pallas kernels, on_device(): pl.pallas_call(pack_kernel, out_shape=jax.ShapeDtypeStruct((PEERS, CHUNK,...  3.92 us
    pallas_call x1, Pallas kernels, on_device(): pl.pallas_call(slab_kernel, out_shape=jax.ShapeDtypeStruct((PEERS, 2 * SL...  3.76 us
    pallas_call x1, Pallas kernels, on_device(): pl.pallas_call(refine_kernel, out_shape=jax.ShapeDtypeStruct((SIDE, 2 * S...  3.12 us
    pallas_call x1, Pallas kernels, on_device(): pl.pallas_call(near_kernel, out_shape=(jax.ShapeDtypeStruct((SIDE // 8, 2...  3.08 us
    ppermute x1, starting transfers between devices, on_device(): lax.ppermute(edge, 'frame', [(i, (i + 1) % frames if i % 2 else (i - 1) %...  2.95 us
  transfers between devices with their start and end apart: 2, of which 1 were waited for; matrix products, arithmetic and copies ran while one was open for 0% of the time, Pallas kernels for 6%

profile of v2, /device:TPU:0, one launch (start us, length us, event | category | flops | bytes accessed | tf_op | source)
XLA Modules:
  0.0 53.2 jit_solution(8372564165905723234)
XLA Ops:
  0.7 0.0 copy-start
  0.7 3.9 %pack.1 = bf16[16,88,384]{2,1,0:T(8,128)(2,1)} custom-call(s32[1]{0:T(128)S(6)} %copy.14.turn_hbm.turn_ref, f32[192,384]{1,0:T(8,128)} %bitcast.8, bf16[12,192,384]{2,1,0:T(8,128)(2,1)} %bitcast.6, bf16[12,48,384]{2,1,0:T(8,128)(2,1)} %bitcast.11, s32[1,192]{1,0:T(1,128)} %mask_ref.1, bf16[768,384]{1,0:T(8,128)(2,1)} %constant.4.clone.w_hbm), custom_call_target="tpu_custom_call" | custom-call | tf_op jit(solution)/shard_map/pack/pallas_call | solution.py:442
  4.6 23.5 %all_to_all.10.got_ref = bf16[16,88,384]{2,1,0:T(8,128)(2,1)S(1)} all-to-all(bf16[16,88,384]{2,1,0:T(8,128)(2,1)} %pack.1), channel_id=1, replica_groups={{0,1,2,3,32,33,34,35,64,65,66,67,96,97,98,99},{4,5,6,7,36,37,38,39,68,6..., dimensions={0} | all-to-all | bytes 2162688 | tf_op jit(solution)/shard_map/all_to_all | solution.py:470
  28.1 0.0 copy-done
  28.1 0.0 copy-start.2
  28.1 0.0 copy-start.3
  28.1 0.0 copy-start.5
  28.1 3.8 %slab.1 = bf16[16,24,384]{2,1,0:T(8,128)(2,1)S(1)} custom-call(bf16[16,88,384]{2,1,0:T(8,128)(2,1)S(1)} %all_to_all.10.got_ref, bf16[6,2,384,384]{3,2,1,0:T(8,128)(2,1)S(1)} %copy-done), custom_call_target="tpu_custom_call" | custom-call | tf_op jit(solution)/shard_map/slab/pallas_call | solution.py:471
  31.9 11.0 %all_to_all.11.back_ref = bf16[16,24,384]{2,1,0:T(8,128)(2,1)S(1)} all-to-all(bf16[16,24,384]{2,1,0:T(8,128)(2,1)S(1)} %slab.1), channel_id=1, replica_groups={{0,1,2,3,32,33,34,35,64,65,66,67,96,97,98,99},{4,5,6,7,36,37,38,39,68,6..., dimensions={0} | all-to-all | bytes 589824 | tf_op jit(solution)/shard_map/all_to_all | solution.py:487
  42.9 0.0 copy-done.2
  42.9 0.3 update.1
  43.2 0.1 collective-permute-start.1
  43.3 3.0 %collective-permute-start = (bf16[192,384]{1,0:T(8,128)(2,1)S(1)}, bf16[192,384]{1,0:T(8,128)(2,1)S(1)}, u32[]{:S(2)}, u32[]{:S(2)}) collective-permute-start(bf16[192,384]{1,0:T(8,128)(2,1)S(1)} %get-tuple-element.10), channel_id=1, source_target_pairs={{0,15},{1,2},{2,1},{3,4},{4,3},{5,6},{6,5},{7,8},{8,7},{9,10},{10,... | collective-permute-start | bytes 442376 | tf_op jit(solution)/shard_map/ppermute | solution.py:501
  46.2 0.0 copy-done.6
  46.2 0.1 copy.13.spatial_ref
  46.3 0.0 collective-permute-done.1.core_ref
  46.3 0.0 copy-done.1
  46.3 0.0 copy-done.3
  46.3 0.0 copy-done.5
  46.3 0.0 copy-start.4
  46.4 3.1 %near.1 = (f32[24,256,192]{2,1,0:T(8,128)S(1)}, bf16[256,192]{1,0:T(8,128)(2,1)S(1)}, f32[192,384]{1,0:T(8,128)S(1)}) custom-call(bf16[192,384]{1,0:T(8,128)(2,1)S(1)} %collective-permute-done.1.core_ref, f32[192,384]{1,0:T(8,128)S(1)} %get-tuple-element.11.own_ref, f32[192,384]{1,0:T(8,128)S(1)} %bitcast.10, s32[1,192]{1,0:T(1,128)S(1)} %copy-done.3, ...), custom_call_target="tpu_custom_call" | custom-call | flops 1132462080 | bytes 6291456 | tf_op jit(solution)/shard_map/near/pallas_call | solution.py:504
  49.4 0.6 %collective-permute-done.chip_ref = bf16[192,384]{1,0:T(8,128)(2,1)S(1)} collective-permute-done((bf16[192,384]{1,0:T(8,128)(2,1)S(1)}, bf16[192,384]{1,0:T(8,128)(2,1)S(1)}, u32[]{:S(2)}, u32[]{:S(2)}) %collective-permute-start) | collective-permute-done | bytes 147488 | tf_op jit(solution)/shard_map/ppermute | solution.py:501
  50.1 0.0 copy-done.4
  50.1 3.1 %refine.1 = f32[192,384]{1,0:T(8,128)} custom-call(bf16[192,384]{1,0:T(8,128)(2,1)S(1)} %collective-permute-done.chip_ref, f32[192,384]{1,0:T(8,128)S(1)} %get-tuple-element.12.own_ref, f32[24,256,192]{2,1,0:T(8,128)S(1)} %get-tuple-element.13.acc_ref, bf16[256,192]{1,0:T(8,128)(2,1)S(1)} %get-tuple-element.14.m_ref, f32[2,32]{1,0:T(2,128)S(1)} %copy-done.4), custom_call_target="tpu_custom_call" | custom-call | tf_op jit(solution)/shard_map/refine/pallas_call | solution.py:529
  (4 shorter events, 0.0 us)
Async XLA Ops:
  0.7 27.4 %copy-start = (bf16[6,2,384,384]{3,2,1,0:T(8,128)(2,1)S(1)}, bf16[6,2,384,384]{3,2,1,0:T(8,128)(2,1)}, u32[]{:S(2)}) copy-start(bf16[6,2,384,384]{3,2,1,0:T(8,128)(2,1)} %constant.5.clone.a_ref) | copy-start | bytes 10616836
  28.1 14.8 %copy-start.2 = (f32[1,1,192,384]{3,2,1,0:T(8,128)S(1)}, f32[1,1,192,384]{3,2,1,0:T(8,128)}, u32[]{:S(2)}) copy-start(f32[1,1,192,384]{3,2,1,0:T(8,128)} %param.10) | copy-start | bytes 884740
  28.1 18.1 %copy-start.6 = (f32[32,2,3,3]{0,1,3,2:T(2,128)S(1)}, f32[32,2,3,3]{0,1,3,2:T(2,128)}, u32[]{:S(2)}) copy-start(f32[32,2,3,3]{0,1,3,2:T(2,128)} %param.15) | copy-start | bytes 6916
  28.1 18.2 %copy-start.1 = (bf16[1,12,192,384]{3,2,1,0:T(8,128)(2,1)S(1)}, bf16[1,12,192,384]{3,2,1,0:T(8,128)(2,1)}, u32[]{:S(2)}) copy-start(bf16[1,12,192,384]{3,2,1,0:T(8,128)(2,1)} %param.11) | copy-start | bytes 5308420
  28.1 18.2 %copy-start.3 = (s32[1,192]{1,0:T(1,128)S(1)}, s32[1,192]{1,0:T(1,128)}, u32[]{:S(2)}) copy-start(s32[1,192]{1,0:T(1,128)} %mask_ref.1) | copy-start | bytes 2308
  28.1 18.2 %copy-start.5 = (f32[3,32,32]{2,1,0:T(8,128)S(1)}, f32[3,32,32]{2,1,0:T(8,128)}, u32[]{:S(2)}) copy-start(f32[3,32,32]{2,1,0:T(8,128)} %temporal_ref.1) | copy-start | bytes 36868
  43.2 3.2 %collective-permute-start.1 = (bf16[192,384]{1,0:T(8,128)(2,1)S(1)}, bf16[192,384]{1,0:T(8,128)(2,1)S(1)}, u32[]{:S(2)}, u32[]{:S(2)}) collective-permute-start(bf16[192,384]{1,0:T(8,128)(2,1)S(1)} %get-tuple-element.10), channel_id=1, source_target_pairs={{0,1},{1,0},{2,3},{3,2},{4,5},{5,4},{6,7},{7,6},{8,9},{9,8},{10,11... | collective-permute-start | bytes 442376 | tf_op jit(solution)/shard_map/ppermute | solution.py:500
  43.3 6.8 %collective-permute-start = (bf16[192,384]{1,0:T(8,128)(2,1)S(1)}, bf16[192,384]{1,0:T(8,128)(2,1)S(1)}, u32[]{:S(2)}, u32[]{:S(2)}) collective-permute-start(bf16[192,384]{1,0:T(8,128)(2,1)S(1)} %get-tuple-element.10), channel_id=1, source_target_pairs={{0,15},{1,2},{2,1},{3,4},{4,3},{5,6},{6,5},{7,8},{8,7},{9,10},{10,... | collective-permute-start | bytes 442376 | tf_op jit(solution)/shard_map/ppermute | solution.py:501
  46.3 3.7 %copy-start.4 = (f32[2,32]{1,0:T(2,128)S(1)}, f32[2,32]{1,0:T(2,128)}, u32[]{:S(2)}) copy-start(f32[2,32]{1,0:T(2,128)} %p_ref.1) | copy-start | bytes 772

commit v3 on v2

--- a/solution.py
+++ b/solution.py
@@ -156,7 +156,7 @@
     return [value[8 * t : 8 * t + 8] for t in range(value.shape[0] // 8)]
 
 
-def slab_kernel(got_ref, a_ref, out_hbm, xs, cs, zs, ys, out_ref, sems):
+def slab_kernel(got_ref, a_ref, out_ref, xs, cs, zs, ys):
     left = lax.broadcasted_iota(jnp.int32, (8, 128), 1) < 64
     lane = lax.broadcasted_iota(jnp.int32, (8, 128), 1)
     low16 = (lane < 16) | ((lane >= 64) & (lane < 80))
@@ -265,9 +265,6 @@
             out_ref[i] = jnp.concatenate(
                 [main_hi, main - main_hi, half_hi, half - half_hi], 0
             ).astype(BF16)
-            pltpu.make_async_copy(out_ref.at[i], out_hbm.at[i], sems.at[i]).start()
-    for i in range(PEERS):
-        pltpu.make_async_copy(out_ref.at[i], out_hbm.at[i], sems.at[i]).wait()
 
 
 def lost_part(x, mask, maps_ref):
@@ -472,14 +469,12 @@
         slab_kernel,
         out_shape=jax.ShapeDtypeStruct((PEERS, 2 * SLAB, 2 * SIDE), BF16),
         in_specs=[VMEM, VMEM],
-        out_specs=HBM,
+        out_specs=VMEM,
         scratch_shapes=[
             pltpu.VMEM((PEERS, 2, 8, 512), F32),
             pltpu.VMEM((PEERS, 5, 8, 512), F32),
             pltpu.VMEM((MB, 40 * G, 2 * SIDE), F32),
             pltpu.VMEM((MB, 40 * G, 512), F32),
-            pltpu.VMEM((PEERS, 2 * SLAB, 2 * SIDE), BF16),
-            pltpu.SemaphoreType.DMA((PEERS,)),
         ],
         compiler_params=params(32),
         name="slab",

time: 53.4 us -> 52.7 us (0.987)
  Pallas kernels: 14.2 us -> 13.4 us
    pallas_call x1, Pallas kernels: 3.76 us -> 2.98 us  [on_device(): pl.pallas_call(slab_kernel, out_shape=jax.ShapeDtypeStruct((PEERS, 2 * SL...]
where the time goes in v3:
time: 52.7 us; the launch traced here: 52.4 us
  blocking collectives  34.5 us (65%)
  Pallas kernels  13.4 us (25%)
  starting transfers between devices  3.04 us (6%)
  between operations  0.75 us (1%)
  waiting for transfers between devices  0.63 us (1%)
    all_to_all x1, blocking collectives, on_device(): got = lax.all_to_all(send, ('cuts', 'frame'), 0, 0, axis_index_groups=where)  23.5 us
    all_to_all x1, blocking collectives, on_device(): lax.all_to_all(slab, ('cuts', 'frame'), 0, 0, axis_index_groups=where)  11 us
    pallas_call x1, Pallas kernels, on_device(): pl.pallas_call(pack_kernel, out_shape=jax.ShapeDtypeStruct((PEERS, CHUNK,...  3.92 us
    pallas_call x1, Pallas kernels, on_device(): pl.pallas_call(refine_kernel, out_shape=jax.ShapeDtypeStruct((SIDE, 2 * S...  3.12 us
    pallas_call x1, Pallas kernels, on_device(): pl.pallas_call(near_kernel, out_shape=(jax.ShapeDtypeStruct((SIDE // 8, 2...  3.08 us
    pallas_call x1, Pallas kernels, on_device(): pl.pallas_call(slab_kernel, out_shape=jax.ShapeDtypeStruct((PEERS, 2 * SL...  2.98 us
    ppermute x1, starting transfers between devices, on_device(): lax.ppermute(edge, 'frame', [(i, (i + 1) % frames if i % 2 else (i - 1) %...  2.96 us
  transfers between devices with their start and end apart: 2, of which 1 were waited for; matrix products, arithmetic and copies ran while one was open for 0% of the time, Pallas kernels for 6%

profile of v3, /device:TPU:0, one launch (start us, length us, event | category | flops | bytes accessed | tf_op | source)
XLA Modules:
  0.0 52.4 jit_solution(2856569766489725984)
XLA Ops:
  0.7 0.0 copy-start
  0.7 3.9 %pack.1 = bf16[16,88,384]{2,1,0:T(8,128)(2,1)} custom-call(s32[1]{0:T(128)S(6)} %copy.14.turn_hbm.turn_ref, f32[192,384]{1,0:T(8,128)} %bitcast.8, bf16[12,192,384]{2,1,0:T(8,128)(2,1)} %bitcast.6, bf16[12,48,384]{2,1,0:T(8,128)(2,1)} %bitcast.11, s32[1,192]{1,0:T(1,128)} %mask_ref.1, bf16[768,384]{1,0:T(8,128)(2,1)} %constant.4.clone.w_hbm), custom_call_target="tpu_custom_call" | custom-call | tf_op jit(solution)/shard_map/pack/pallas_call | solution.py:439
  4.6 23.5 %all_to_all.10.got_ref = bf16[16,88,384]{2,1,0:T(8,128)(2,1)S(1)} all-to-all(bf16[16,88,384]{2,1,0:T(8,128)(2,1)} %pack.1), channel_id=1, replica_groups={{0,1,2,3,32,33,34,35,64,65,66,67,96,97,98,99},{4,5,6,7,36,37,38,39,68,6..., dimensions={0} | all-to-all | bytes 2162688 | tf_op jit(solution)/shard_map/all_to_all | solution.py:467
  28.1 0.0 copy-done
  28.1 0.0 copy-start.2
  28.1 0.0 copy-start.3
  28.1 0.0 copy-start.5
  28.1 3.0 %slab.1 = bf16[16,24,384]{2,1,0:T(8,128)(2,1)S(1)} custom-call(bf16[16,88,384]{2,1,0:T(8,128)(2,1)S(1)} %all_to_all.10.got_ref, bf16[6,2,384,384]{3,2,1,0:T(8,128)(2,1)S(1)} %copy-done), custom_call_target="tpu_custom_call" | custom-call | tf_op jit(solution)/shard_map/slab/pallas_call | solution.py:468
  31.1 11.0 %all_to_all.11.back_ref = bf16[16,24,384]{2,1,0:T(8,128)(2,1)S(1)} all-to-all(bf16[16,24,384]{2,1,0:T(8,128)(2,1)S(1)} %slab.1), channel_id=1, replica_groups={{0,1,2,3,32,33,34,35,64,65,66,67,96,97,98,99},{4,5,6,7,36,37,38,39,68,6..., dimensions={0} | all-to-all | bytes 589824 | tf_op jit(solution)/shard_map/all_to_all | solution.py:482
  42.1 0.0 copy-done.2
  42.1 0.3 update.1
  42.4 0.1 collective-permute-start.1
  42.5 3.0 %collective-permute-start = (bf16[192,384]{1,0:T(8,128)(2,1)S(1)}, bf16[192,384]{1,0:T(8,128)(2,1)S(1)}, u32[]{:S(2)}, u32[]{:S(2)}) collective-permute-start(bf16[192,384]{1,0:T(8,128)(2,1)S(1)} %get-tuple-element.10), channel_id=1, source_target_pairs={{0,15},{1,2},{2,1},{3,4},{4,3},{5,6},{6,5},{7,8},{8,7},{9,10},{10,... | collective-permute-start | bytes 442376 | tf_op jit(solution)/shard_map/ppermute | solution.py:496
  45.4 0.0 copy-done.6
  45.5 0.1 copy.13.spatial_ref
  45.5 0.0 collective-permute-done.1.core_ref
  45.5 0.0 copy-done.1
  45.5 0.0 copy-done.3
  45.6 0.0 copy-done.5
  45.6 0.0 copy-start.4
  45.6 3.1 %near.1 = (f32[24,256,192]{2,1,0:T(8,128)S(1)}, bf16[256,192]{1,0:T(8,128)(2,1)S(1)}, f32[192,384]{1,0:T(8,128)S(1)}) custom-call(bf16[192,384]{1,0:T(8,128)(2,1)S(1)} %collective-permute-done.1.core_ref, f32[192,384]{1,0:T(8,128)S(1)} %get-tuple-element.11.own_ref, f32[192,384]{1,0:T(8,128)S(1)} %bitcast.10, s32[1,192]{1,0:T(1,128)S(1)} %copy-done.3, ...), custom_call_target="tpu_custom_call" | custom-call | flops 1132462080 | bytes 6291456 | tf_op jit(solution)/shard_map/near/pallas_call | solution.py:499
  48.7 0.6 %collective-permute-done.chip_ref = bf16[192,384]{1,0:T(8,128)(2,1)S(1)} collective-permute-done((bf16[192,384]{1,0:T(8,128)(2,1)S(1)}, bf16[192,384]{1,0:T(8,128)(2,1)S(1)}, u32[]{:S(2)}, u32[]{:S(2)}) %collective-permute-start) | collective-permute-done | bytes 147488 | tf_op jit(solution)/shard_map/ppermute | solution.py:496
  49.3 0.0 copy-done.4
  49.3 3.1 %refine.1 = f32[192,384]{1,0:T(8,128)} custom-call(bf16[192,384]{1,0:T(8,128)(2,1)S(1)} %collective-permute-done.chip_ref, f32[192,384]{1,0:T(8,128)S(1)} %get-tuple-element.12.own_ref, f32[24,256,192]{2,1,0:T(8,128)S(1)} %get-tuple-element.13.acc_ref, bf16[256,192]{1,0:T(8,128)(2,1)S(1)} %get-tuple-element.14.m_ref, f32[2,32]{1,0:T(2,128)S(1)} %copy-done.4), custom_call_target="tpu_custom_call" | custom-call | tf_op jit(solution)/shard_map/refine/pallas_call | solution.py:524
  (4 shorter events, 0.0 us)
Async XLA Ops:
  0.7 27.4 %copy-start = (bf16[6,2,384,384]{3,2,1,0:T(8,128)(2,1)S(1)}, bf16[6,2,384,384]{3,2,1,0:T(8,128)(2,1)}, u32[]{:S(2)}) copy-start(bf16[6,2,384,384]{3,2,1,0:T(8,128)(2,1)} %constant.5.clone.a_ref) | copy-start | bytes 10616836
  28.1 14.0 %copy-start.2 = (f32[1,1,192,384]{3,2,1,0:T(8,128)S(1)}, f32[1,1,192,384]{3,2,1,0:T(8,128)}, u32[]{:S(2)}) copy-start(f32[1,1,192,384]{3,2,1,0:T(8,128)} %param.10) | copy-start | bytes 884740
  28.1 17.3 %copy-start.6 = (f32[32,2,3,3]{0,1,3,2:T(2,128)S(1)}, f32[32,2,3,3]{0,1,3,2:T(2,128)}, u32[]{:S(2)}) copy-start(f32[32,2,3,3]{0,1,3,2:T(2,128)} %param.15) | copy-start | bytes 6916
  28.1 17.5 %copy-start.1 = (bf16[1,12,192,384]{3,2,1,0:T(8,128)(2,1)S(1)}, bf16[1,12,192,384]{3,2,1,0:T(8,128)(2,1)}, u32[]{:S(2)}) copy-start(bf16[1,12,192,384]{3,2,1,0:T(8,128)(2,1)} %param.11) | copy-start | bytes 5308420
  28.1 17.4 %copy-start.3 = (s32[1,192]{1,0:T(1,128)S(1)}, s32[1,192]{1,0:T(1,128)}, u32[]{:S(2)}) copy-start(s32[1,192]{1,0:T(1,128)} %mask_ref.1) | copy-start | bytes 2308
  28.1 17.4 %copy-start.5 = (f32[3,32,32]{2,1,0:T(8,128)S(1)}, f32[3,32,32]{2,1,0:T(8,128)}, u32[]{:S(2)}) copy-start(f32[3,32,32]{2,1,0:T(8,128)} %temporal_ref.1) | copy-start | bytes 36868
  42.4 3.2 %collective-permute-start.1 = (bf16[192,384]{1,0:T(8,128)(2,1)S(1)}, bf16[192,384]{1,0:T(8,128)(2,1)S(1)}, u32[]{:S(2)}, u32[]{:S(2)}) collective-permute-start(bf16[192,384]{1,0:T(8,128)(2,1)S(1)} %get-tuple-element.10), channel_id=1, source_target_pairs={{0,1},{1,0},{2,3},{3,2},{4,5},{5,4},{6,7},{7,6},{8,9},{9,8},{10,11... | collective-permute-start | bytes 442376 | tf_op jit(solution)/shard_map/ppermute | solution.py:495
  42.5 6.8 %collective-permute-start = (bf16[192,384]{1,0:T(8,128)(2,1)S(1)}, bf16[192,384]{1,0:T(8,128)(2,1)S(1)}, u32[]{:S(2)}, u32[]{:S(2)}) collective-permute-start(bf16[192,384]{1,0:T(8,128)(2,1)S(1)} %get-tuple-element.10), channel_id=1, source_target_pairs={{0,15},{1,2},{2,1},{3,4},{4,3},{5,6},{6,5},{7,8},{8,7},{9,10},{10,... | collective-permute-start | bytes 442376 | tf_op jit(solution)/shard_map/ppermute | solution.py:496
  45.6 3.7 %copy-start.4 = (f32[2,32]{1,0:T(2,128)S(1)}, f32[2,32]{1,0:T(2,128)}, u32[]{:S(2)}) copy-start(f32[2,32]{1,0:T(2,128)} %p_ref.1) | copy-start | bytes 772
